TPU v7x, 128 devices: a whole 4x4x4 slice. The times are simulated.
128 devices in a mesh: wide: 8 (over z, core), narrow: 16 (over y, x).
Axes of the slice: x: 4, y: 4, z: 4, core: 2. Of those that a mesh axis runs over, the one named last changes fastest.
Arguments:
- source: float32 [128, 512, 128], P('wide', 'narrow'), may hold values from -8 to 8
- conduct: float32 [128, 512, 128], P('wide', 'narrow'), may hold values from 0.5 to 2
- storage: float32 [128, 512, 128], P('wide', 'narrow'), may hold values from 0.25 to 2
Outputs:
- correction: float32 [128, 512, 128], P('wide', 'narrow')
- remainder: float32 [128, 512, 128], P('wide', 'narrow')
- upper: float32 [9, 9], replicated
- residual_norm: float32 [], replicated
All inputs are finite; a program needn't handle non-finite values.
Results may differ from a plain program's by a relative error of at most 0.039.
Values sent between devices are 32-bit elements; how exact they have to be, the bound alone decides.
No kernel may reach another device: no remote copies, remote signals or barrier semaphores. Data moves between devices by JAX's collectives and lax.ppermute only.
A program may use at most 128 MiB of HBM per device.

v0:
```python
import math

import jax
import jax.numpy as jnp
from jax import lax
from jax.experimental import pallas as pl
from jax.experimental.pallas import tpu as pltpu
from jax.sharding import PartitionSpec as P

STEPS = 8
COLS = 9
HALO = 8

leja_order = (0, 7, 3, 5, 2, 6, 1, 4)
spread_scale = 6.5
MIB = 1024 * 1024


def newton_shifts():
    return [
        13.125 + 12.875 * math.cos(math.pi * (2 * position + 1) / 16.0) for position in leja_order
    ]


def is_odd(axis):
    return lax.rem(lax.axis_index(axis), 2) == 1


def exchange(first, second, axis):
    size = lax.axis_size(axis)
    inner = [(i, i ^ 1) for i in range(size)]
    outer = [(i, (((i + 1) % size ^ 1) - 1) % size) for i in range(size)]
    return lax.ppermute(first, axis, inner), lax.ppermute(second, axis, outer)


def vmem_spec(count):
    return [pl.BlockSpec(memory_space=pltpu.VMEM)] * count


def edge_kernel(source, conduct, storage, inner, outer, own, sems):
    odd = is_odd("narrow")
    width = source.shape[1]

    def fill(low, high):
        copies = []
        for k, ref in enumerate((source, conduct, storage)):
            for side, (at, out) in enumerate(((0, low), (width - HALO, high))):
                copies.append(
                    pltpu.make_async_copy(
                        ref.at[:, pl.ds(at, HALO), :], out.at[k], sems.at[2 * k + side]
                    )
                )
            copies.append(pltpu.make_async_copy(ref, own.at[k], sems.at[6 + k]))
        for copy in copies:
            copy.start()
        for copy in copies:
            copy.wait()

    @pl.when(odd)
    def _():
        fill(inner, outer)

    @pl.when(jnp.logical_not(odd))
    def _():
        fill(outer, inner)


def edges(source, conduct, storage):
    size_x, _, size_z = source.shape
    shape = jax.ShapeDtypeStruct((3, size_x, HALO, size_z), jnp.float32)
    whole = jax.ShapeDtypeStruct((3, *source.shape), jnp.float32)
    return pl.pallas_call(
        edge_kernel,
        out_shape=(shape, shape, whole),
        in_specs=[pl.BlockSpec(memory_space=pltpu.HBM)] * 3,
        out_specs=tuple(vmem_spec(3)),
        scratch_shapes=[pltpu.SemaphoreType.DMA((9,))],
        compiler_params=pltpu.CompilerParams(vmem_limit_bytes=8 * MIB),
        name="edges",
    )(*(pltpu.with_memory_space_constraint(x, pltpu.HBM) for x in (source, conduct, storage)))


def widen_kernel(last, own, inner, outer, near, far):
    odd_n, odd_w = is_odd("narrow"), is_odd("wide")
    place = lax.axis_index("narrow")
    keep_low = jnp.where(place == 0, 0.0, 1.0)
    keep_high = jnp.where(place == last, 0.0, 1.0)
    _, size_x, width, _ = own.shape
    half = size_x // 2

    def fill(low_rows, high_rows, low_half, high_half):
        for k in range(3):
            for part, out in ((0, low_half), (1, high_half)):
                cells = slice(part * half, (part + 1) * half)
                out[k, :, 0:HALO, :] = low_rows[k, cells] * keep_low
                out[k, :, HALO : HALO + width, :] = own[k, cells]
                out[k, :, HALO + width :, :] = high_rows[k, cells] * keep_high

    for flag_n in (False, True):
        for flag_w in (False, True):

            @pl.when(jnp.logical_and(odd_n == flag_n, odd_w == flag_w))
            def _(flag_n=flag_n, flag_w=flag_w):
                rows = (inner, outer) if flag_n else (outer, inner)
                halves = (near, far) if flag_w else (far, near)
                fill(*rows, *halves)


def widen(own, inner, outer):
    _, size_x, width, size_z = own.shape
    shape = jax.ShapeDtypeStruct((3, size_x // 2, width + 2 * HALO, size_z), jnp.float32)
    last = lax.axis_size("narrow") - 1
    return pl.pallas_call(
        lambda *refs: widen_kernel(last, *refs),
        out_shape=(shape, shape),
        in_specs=vmem_spec(3),
        out_specs=tuple(vmem_spec(2)),
        compiler_params=pltpu.CompilerParams(vmem_limit_bytes=8 * MIB),
        name="widen",
    )(own, inner, outer)


def total(x):
    return jnp.sum(jnp.sum(x, axis=0, keepdims=True), axis=1, keepdims=True)


def basis_kernel(
    last, long_y, near, far, inner, outer, basis, rows_out,
    field, cond, diag, face_x, face_y, face_yp, face_z, face_zp,
    back_a, front_a, back_b, front_b, work,
):
    odd_w = is_odd("wide")
    place_w, place_n = lax.axis_index("wide"), lax.axis_index("narrow")
    keep_left = jnp.where(place_w == 0, 0.0, 1.0)
    keep_right = jnp.where(place_w == last[0], 0.0, 1.0)
    keep_low = jnp.where(place_n == 0, 0.0, 1.0)
    keep_high = jnp.where(place_n == last[1], 0.0, 1.0)
    size_z = field.shape[1]
    long_x = field.shape[0] // long_y
    size_x, size_y = long_x - 2 * HALO, long_y - 2 * HALO
    shifts = newton_shifts()

    def at(x, count=long_y, first=0):
        start = x * long_y + first
        if not isinstance(x, int) and first % 8 == 0:
            start = pl.multiple_of(start, 8)
        return pl.ds(start, count)

    def place(parts):
        start = 0
        for part, keep in zip(parts, (keep_left, None, None, keep_right)):
            rows = part.shape[1]
            for k, (out, skip) in enumerate(((field, 0), (cond, long_y), (diag, 0))):
                value = part[k]
                out[pl.ds(start + skip, rows), :] = value if keep is None else value * keep
            start += rows

    @pl.when(odd_w)
    def _():
        place((inner, near, far, outer))

    @pl.when(jnp.logical_not(odd_w))
    def _():
        place((outer, far, near, inner))

    empty = jnp.zeros((long_y, size_z), jnp.float32)
    cond[at(0), :] = empty
    cond[at(long_x + 1), :] = empty

    lane = lax.broadcasted_iota(jnp.int32, (long_y, size_z), 1)
    row = lax.broadcasted_iota(jnp.int32, (long_y, size_z), 0)
    unit = 1.0 / spread_scale
    half = 0.5 * unit
    mask_y = jnp.where(row == HALO, keep_low, jnp.where(row == HALO + size_y, keep_high, 1.0))
    mask_yp = jnp.where(
        row == HALO - 1, keep_low, jnp.where(row == HALO + size_y - 1, keep_high, 1.0)
    )

    def turn(value):
        return (
            jnp.where(lane == 0, 0.0, pltpu.roll(value, 1, 1)),
            jnp.where(lane == size_z - 1, 0.0, pltpu.roll(value, size_z - 1, 1)),
        )

    def turn_start(x):
        here = field[at(x), :]
        back_a[at(x), :] = pltpu.roll(here, 1, 1)
        front_a[at(x), :] = pltpu.roll(here, size_z - 1, 1)
        back, front = turn(cond[at(x + 1), :])
        back_b[at(x), :] = back
        front_b[at(x), :] = front

    def coefficients(x):
        here = cond[at(x + 1), :]
        left = half * (here + cond[at(x), :])
        right = half * (here + cond[at(x + 2), :])
        low = half * (here + cond[at(x + 1, long_y, -1), :])
        high = half * (here + cond[at(x + 1, long_y, 1), :])
        z_low = half * (here + back_b[at(x), :])
        z_high = half * (here + front_b[at(x), :])
        face_x[at(x), :] = left
        face_y[at(x), :] = low * mask_y
        face_yp[at(x), :] = high * mask_yp
        face_z[at(x), :] = jnp.where(lane == 0, 0.0, z_low)
        face_zp[at(x), :] = jnp.where(lane == size_z - 1, 0.0, z_high)
        diag[at(x), :] = unit * diag[at(x), :] + ((left + right) + (low + high) + (z_low + z_high))

    group = 4

    def start_group(g, _):
        for i in range(group):
            coefficients((g - 1) * group + i)
        for i in range(group):
            turn_start(g * group + i)
        return 0

    for i in range(group):
        turn_start(i)
    lax.fori_loop(1, long_x // group, start_group, 0)
    for i in range(group):
        coefficients(long_x - group + i)
    face_x[at(HALO), :] = face_x[at(HALO), :] * keep_left
    face_x[at(HALO + size_x), :] = face_x[at(HALO + size_x), :] * keep_right

    def step(number, read, back, front, write, next_back, next_front):
        theta = shifts[number] * unit
        final = number == STEPS - 1
        low, count = (HALO, size_y) if final else (0, long_y)

        def plane(x):
            rows = at(x, count, low)
            here = read[rows, :]
            beside = (
                face_x[at(x + 1, count, low), :] * read[at(x + 1, count, low), :]
                + face_x[rows, :] * read[at(x - 1, count, low), :]
            )
            across = (
                face_yp[rows, :] * read[at(x, count, low + 1), :]
                + face_y[rows, :] * read[at(x, count, low - 1), :]
            )
            along = face_zp[rows, :] * front[rows, :] + face_z[rows, :] * back[rows, :]
            write[rows, :] = (diag[rows, :] - theta) * here - (beside + across + along)

        def turn_plane(x):
            if not final:
                here = write[at(x), :]
                next_back[at(x), :] = pltpu.roll(here, 1, 1)
                next_front[at(x), :] = pltpu.roll(here, size_z - 1, 1)

        start, stop = number + 1, long_x - 1 - number
        head = (stop - start) % group or group
        for x in range(start, start + head):
            plane(x)
        for x in range(start + 1, start + head):
            turn_plane(x)
        begin = start + head
        for x in range(begin, begin + group):
            plane(x)

        def body(g, _):
            x = begin + g * group
            for i in range(group):
                turn_plane(x - group + i)
            for i in range(group):
                plane(x + i)
            return 0

        lax.fori_loop(1, (stop - begin) // group, body, 0)
        for x in range(stop - group, stop - 1):
            turn_plane(x)

    turned = ((back_a, front_a), (back_b, front_b))
    for number in range(STEPS):
        read = field if number == 0 else basis.at[number - 1]
        step(number, read, *turned[number % 2], basis.at[number], *turned[(number + 1) % 2])

    def own(x):
        return at(x + HALO, size_y, HALO)

    def fold(product):
        parts = [product[8 * t : 8 * t + 8] for t in range(size_y // 8)]
        while len(parts) > 1:
            parts = [a + b for a, b in zip(parts[::2], parts[1::2])]
        return parts[0]

    zero = jnp.zeros((8, size_z), jnp.float32)

    def first_dots(x, sums):
        columns = [field[own(x), :]] + [basis[j, own(x), :] for j in range(STEPS)]
        return tuple(s + fold(columns[0] * c) for s, c in zip(sums, columns))

    sums = lax.fori_loop(0, size_x, first_dots, (zero,) * COLS)
    dots = [total(s) for s in sums]
    index = lax.broadcasted_iota(jnp.int32, (1, 128), 1)
    packed = jnp.zeros((1, 128), jnp.float32)
    for k in range(COLS):
        length = jnp.sqrt(dots[0])
        inverse = jnp.where(dots[0] > 0.0, 1.0 / length, 0.0)
        ratio = [d * inverse * inverse for d in dots]
        for j in range(k, COLS):
            entry = length if j == k else dots[j - k] * inverse
            packed = jnp.where(index == 8 * j + k, entry, packed)
        if k == COLS - 1:
            break

        def sweep(x, sums, k=k, ratio=ratio):
            pivot = field[own(x), :] if k == 0 else work[k, x]
            columns = []
            for j in range(k + 1, COLS):
                old = basis[j - 1, own(x), :] if k == 0 else work[j, x]
                new = old - ratio[j - k] * pivot
                work[j, x] = new
                columns.append(new)
            return tuple(s + fold(columns[0] * c) for s, c in zip(sums, columns))

        sums = lax.fori_loop(0, size_x, sweep, (zero,) * (COLS - 1 - k))
        dots = [total(s) for s in sums]
    rows_out[...] = jnp.broadcast_to(packed, rows_out.shape)


def basis_and_factor(near, far, inner, outer):
    _, half, long_y, size_z = near.shape
    size_x, size_y = 2 * half, long_y - 2 * HALO
    long_x = size_x + 2 * HALO
    devices = lax.axis_size("wide") * lax.axis_size("narrow")
    last = (lax.axis_size("wide") - 1, lax.axis_size("narrow") - 1)
    flat = lambda x: x.reshape(3, half * long_y, size_z)
    planes = lambda count: pltpu.VMEM((count * long_y, size_z), jnp.float32)
    return pl.pallas_call(
        lambda *refs: basis_kernel(last, long_y, *refs),
        out_shape=(
            jax.ShapeDtypeStruct((STEPS, long_x * long_y, size_z), jnp.float32),
            jax.ShapeDtypeStruct((devices, 128), jnp.float32),
        ),
        in_specs=vmem_spec(4),
        out_specs=tuple(vmem_spec(2)),
        scratch_shapes=[planes(long_x), planes(long_x + 2)] + [planes(long_x)] * 10
        + [pltpu.VMEM((COLS, size_x, size_y, size_z), jnp.float32)],
        compiler_params=pltpu.CompilerParams(vmem_limit_bytes=28 * MIB),
        name="basis_and_factor",
    )(flat(near), flat(far), flat(inner), flat(outer))


def split(x):
    big = x * 4097.0
    high = big - (big - x)
    return high, x - high


def two_sum(a, b):
    s = a + b
    t = s - a
    return s, (a - (s - t)) + (b - t)


def small_solve(factor):
    shifts = newton_shifts()
    null = [1.0]
    for theta in shifts:
        null.append(-theta / spread_scale * null[-1])
    inverse = [1.0 / factor[(i, i)] for i in range(COLS)]

    left = [jnp.full((1, 1), w, jnp.float32) for w in null]
    normal = []
    for i in range(COLS):
        normal.append(left[i] * inverse[i])
        for j in range(i + 1, COLS):
            left[j] = left[j] - factor[(i, j)] * normal[i]
    square = normal[0] * normal[0]
    for i in range(1, COLS):
        square = square + normal[i] * normal[i]
    target = [entry / square for entry in normal]

    def back(right):
        right, solved = list(right), [None] * COLS
        for j in range(COLS - 1, -1, -1):
            solved[j] = right[j] * inverse[j]
            for i in range(j):
                right[i] = right[i] - factor[(i, j)] * solved[j]
        return solved

    z = back(target)
    z_parts = [split(entry) for entry in z]
    missing = []
    for i in range(COLS):
        high, low = target[i], None
        for j in range(i, COLS):
            (ah, al), (bh, bl) = split(factor[(i, j)]), z_parts[j]
            product = factor[(i, j)] * z[j]
            error = ((ah * bh - product) + ah * bl + al * bh) + al * bl
            high, carry = two_sum(high, -product)
            carry = carry - error
            low = carry if low is None else low + carry
        missing.append(high + low)
    z = [a + b for a, b in zip(z, back(missing))]

    y = [None] * STEPS
    for j in range(STEPS, 0, -1):
        right = -z[j]
        if j < STEPS:
            right = right - shifts[j] * y[j]
        y[j - 1] = right * (1.0 / spread_scale)
    return y, 1.0 / jnp.sqrt(square), z


def combine_kernel(own, basis, rows, correction, remainder, upper, norm):
    stacked = rows[...].T
    tops = [stacked[8 * j : 8 * j + 8] for j in range(COLS)]
    tail = stacked[8 * COLS : 8 * COLS + 8]
    sublane = lax.broadcasted_iota(jnp.int32, (8, 128), 0)
    tail = jnp.where(sublane == 0, tail, 0.0)
    factor = {}
    for k in range(COLS):
        square = tops[k] * tops[k]
        if k == COLS - 1:
            square = square + tail * tail
        dots = [total(square)] + [total(tops[k] * tops[j]) for j in range(k + 1, COLS)]
        ridge = dots[0] + 1e-12
        length = jnp.sqrt(ridge)
        again = 2.0 - dots[0] / ridge
        factor[(k, k)] = length
        for j in range(k + 1, COLS):
            factor[(k, j)] = dots[j - k] / length * again
            tops[j] = tops[j] - (dots[j - k] / ridge * again) * tops[k]

    y, size, z = small_solve(factor)

    line = lax.broadcasted_iota(jnp.int32, (16, 128), 0)
    lane = lax.broadcasted_iota(jnp.int32, (16, 128), 1)
    table = jnp.zeros((16, 128), jnp.float32)
    for (i, j), entry in factor.items():
        table = jnp.where(jnp.logical_and(line == i, lane == j), entry, table)
    upper[...] = table[:COLS, :COLS]
    norm[...] = size

    _, size_x, size_y, _ = own.shape
    long_y = size_y + 2 * HALO

    def combine(x, _):
        here = own[0, x]
        first, second = y[0] * here, z[0] * here
        for j in range(1, COLS):
            here = basis[j - 1, pl.ds(pl.multiple_of((x + HALO) * long_y + HALO, 8), size_y), :]
            if j < STEPS:
                first = first + y[j] * here
            second = second + z[j] * here
        correction[x] = first
        remainder[x] = second
        return 0

    lax.fori_loop(0, size_x, combine, 0)


def combine(own, basis, rows):
    block = jax.ShapeDtypeStruct(own.shape[1:], jnp.float32)
    return pl.pallas_call(
        combine_kernel,
        out_shape=(
            block,
            block,
            jax.ShapeDtypeStruct((COLS, COLS), jnp.float32),
            jax.ShapeDtypeStruct((1, 1), jnp.float32),
        ),
        in_specs=vmem_spec(3),
        out_specs=tuple(vmem_spec(4)),
        compiler_params=pltpu.CompilerParams(vmem_limit_bytes=8 * MIB),
        name="combine",
    )(own, basis, rows)


def on_device(source, conduct, storage):
    inner, outer, own = edges(source, conduct, storage)
    near, far = widen(own, *exchange(inner, outer, "narrow"))
    planes = exchange(near, far, "wide")
    basis, packed = basis_and_factor(near, far, *planes)
    gathered = lax.all_to_all(packed, ("wide", "narrow"), 0, 0, tiled=True)
    correction, remainder, factor, resid = combine(own, basis, gathered)
    return correction, remainder, factor, resid[0, 0]


def solution(mesh):
    spec = P("wide", "narrow", None)
    return jax.shard_map(
        on_device,
        mesh=mesh,
        in_specs=(spec, spec, spec),
        out_specs=(spec, spec, P(), P()),
        check_vma=False,
    )
```

profile of v0, /device:TPU:1, one launch (start us, length us, event | category | flops | bytes accessed | tf_op | source)
XLA Modules:
  0.0 57.3 jit_solution(3522426695658992034)
XLA Ops:
  0.6 1.4 %edges.1 = (f32[3,16,8,128]{3,2,1,0:T(8,128)S(1)}, f32[3,16,8,128]{3,2,1,0:T(8,128)S(1)}, f32[3,16,32,128]{3,2,1,0:T(8,128)S(1)}) custom-call(f32[16,32,128]{2,1,0:T(8,128)} %source.1, f32[16,32,128]{2,1,0:T(8,128)} %conduct.1, f32[16,32,128]{2,1,0:T(8,128)} %storage.1), custom_call_target="tpu_custom_call" | custom-call | tf_op jit(solution)/shard_map/edges/pallas_call | solution.py:72
  2.0 2.1 %collective-permute-start = (f32[3,16,8,128]{3,2,1,0:T(8,128)S(1)}, f32[3,16,8,128]{3,2,1,0:T(8,128)S(1)}, u32[]{:S(2)}, u32[]{:S(2)}) collective-permute-start(f32[3,16,8,128]{3,2,1,0:T(8,128)S(1)} %get-tuple-element.16), channel_id=1, source_target_pairs={{0,1},{1,0},{2,3},{3,2},{4,5},{5,4},{6,7},{7,6},{8,9},{9,8},{10,11... | collective-permute-start | bytes 589832 | tf_op jit(solution)/shard_map/ppermute | solution.py:33
  4.1 4.3 %collective-permute-start.1 = (f32[3,16,8,128]{3,2,1,0:T(8,128)S(1)}, f32[3,16,8,128]{3,2,1,0:T(8,128)S(1)}, u32[]{:S(2)}, u32[]{:S(2)}) collective-permute-start(f32[3,16,8,128]{3,2,1,0:T(8,128)S(1)} %get-tuple-element.17), channel_id=1, source_target_pairs={{0,15},{1,2},{2,1},{3,4},{4,3},{5,6},{6,5},{7,8},{8,7},{9,10},{10,... | collective-permute-start | bytes 589832 | tf_op jit(solution)/shard_map/ppermute | solution.py:33
  8.4 0.0 collective-permute-done.refs_1_
  8.4 4.5 %collective-permute-done.1.refs_2_ = f32[3,16,8,128]{3,2,1,0:T(8,128)S(1)} collective-permute-done((f32[3,16,8,128]{3,2,1,0:T(8,128)S(1)}, f32[3,16,8,128]{3,2,1,0:T(8,128)S(1)}, u32[]{:S(2)}, u32[]{:S(2)}) %collective-permute-start.1) | collective-permute-done | bytes 196640 | tf_op jit(solution)/shard_map/ppermute | solution.py:33
  12.9 0.1 widen.1
  13.0 1.9 %collective-permute-start.2 = (f32[3,8,48,128]{3,2,1,0:T(8,128)S(1)}, f32[3,8,48,128]{3,2,1,0:T(8,128)S(1)}, u32[]{:S(2)}, u32[]{:S(2)}) collective-permute-start(f32[3,8,48,128]{3,2,1,0:T(8,128)S(1)} %get-tuple-element.18), channel_id=1, source_target_pairs={{0,16},{16,0},{32,48},{48,32},{64,80},{80,64},{96,112},{112,96},{1... | collective-permute-start | bytes 1769480 | tf_op jit(solution)/shard_map/ppermute | solution.py:33
  15.0 1.6 %collective-permute-start.3 = (f32[3,8,48,128]{3,2,1,0:T(8,128)S(1)}, f32[3,8,48,128]{3,2,1,0:T(8,128)S(1)}, u32[]{:S(2)}, u32[]{:S(2)}) collective-permute-start(f32[3,8,48,128]{3,2,1,0:T(8,128)S(1)} %get-tuple-element.19), channel_id=1, source_target_pairs={{0,112},{16,32},{32,16},{48,64},{64,48},{80,96},{96,80},{112,0},{1... | collective-permute-start | bytes 1769480 | tf_op jit(solution)/shard_map/ppermute | solution.py:33
  16.6 0.0 collective-permute-done.2
  16.6 8.0 %collective-permute-done.3 = f32[3,8,48,128]{3,2,1,0:T(8,128)S(1)} collective-permute-done((f32[3,8,48,128]{3,2,1,0:T(8,128)S(1)}, f32[3,8,48,128]{3,2,1,0:T(8,128)S(1)}, u32[]{:S(2)}, u32[]{:S(2)}) %collective-permute-start.3) | collective-permute-done | bytes 589856 | tf_op jit(solution)/shard_map/ppermute | solution.py:33
  24.6 11.1 %basis_and_factor.1 = (f32[8,1536,128]{2,1,0:T(8,128)S(1)}, f32[128,128]{1,0:T(8,128)S(1)}) custom-call(f32[3,384,128]{2,1,0:T(8,128)S(1)} %bitcast.9, f32[3,384,128]{2,1,0:T(8,128)S(1)} %bitcast.10, f32[3,384,128]{2,1,0:T(8,128)S(1)} %bitcast.11, f32[3,384,128]{2,1,0:T(8,128)S(1)} %bitcast.12), custom_call_target="tpu_custom_call" | custom-call | tf_op jit(solution)/shard_map/basis_and_factor/pallas_call | solution.py:329
  35.6 19.3 %all_to_all.11 = f32[128,1,128]{2,1,0:T(1,128)S(1)} all-to-all(f32[128,1,128]{2,1,0:T(1,128)S(1)} %bitcast.14), channel_id=1, replica_groups=mesh['wide'=8,'narrow'=16] {'wide','narrow'}, dimensions={0} | all-to-all | bytes 131072 | tf_op jit(solution)/shard_map/all_to_all | solution.py:476
  54.9 2.3 %combine.1 = (f32[16,32,128]{2,1,0:T(8,128)}, f32[16,32,128]{2,1,0:T(8,128)}, f32[9,9]{1,0:T(8,128)}, f32[1,1]{1,0:T(1,128)}) custom-call(f32[3,16,32,128]{3,2,1,0:T(8,128)S(1)} %get-tuple-element.15.refs_0_.own, f32[8,1536,128]{2,1,0:T(8,128)S(1)} %get-tuple-element.20.basis, f32[128,128]{1,0:T(8,128)S(1)} %bitcast.13), custom_call_target="tpu_custom_call" | custom-call | tf_op jit(solution)/shard_map/combine/pallas_call | solution.py:456
Async XLA Ops:
  2.0 6.4 %collective-permute-start = (f32[3,16,8,128]{3,2,1,0:T(8,128)S(1)}, f32[3,16,8,128]{3,2,1,0:T(8,128)S(1)}, u32[]{:S(2)}, u32[]{:S(2)}) collective-permute-start(f32[3,16,8,128]{3,2,1,0:T(8,128)S(1)} %get-tuple-element.16), channel_id=1, source_target_pairs={{0,1},{1,0},{2,3},{3,2},{4,5},{5,4},{6,7},{7,6},{8,9},{9,8},{10,11... | collective-permute-start | bytes 589832 | tf_op jit(solution)/shard_map/ppermute | solution.py:33
  4.1 8.8 %collective-permute-start.1 = (f32[3,16,8,128]{3,2,1,0:T(8,128)S(1)}, f32[3,16,8,128]{3,2,1,0:T(8,128)S(1)}, u32[]{:S(2)}, u32[]{:S(2)}) collective-permute-start(f32[3,16,8,128]{3,2,1,0:T(8,128)S(1)} %get-tuple-element.17), channel_id=1, source_target_pairs={{0,15},{1,2},{2,1},{3,4},{4,3},{5,6},{6,5},{7,8},{8,7},{9,10},{10,... | collective-permute-start | bytes 589832 | tf_op jit(solution)/shard_map/ppermute | solution.py:33
  13.0 3.6 %collective-permute-start.2 = (f32[3,8,48,128]{3,2,1,0:T(8,128)S(1)}, f32[3,8,48,128]{3,2,1,0:T(8,128)S(1)}, u32[]{:S(2)}, u32[]{:S(2)}) collective-permute-start(f32[3,8,48,128]{3,2,1,0:T(8,128)S(1)} %get-tuple-element.18), channel_id=1, source_target_pairs={{0,16},{16,0},{32,48},{48,32},{64,80},{80,64},{96,112},{112,96},{1... | collective-permute-start | bytes 1769480 | tf_op jit(solution)/shard_map/ppermute | solution.py:33
  15.0 9.6 %collective-permute-start.3 = (f32[3,8,48,128]{3,2,1,0:T(8,128)S(1)}, f32[3,8,48,128]{3,2,1,0:T(8,128)S(1)}, u32[]{:S(2)}, u32[]{:S(2)}) collective-permute-start(f32[3,8,48,128]{3,2,1,0:T(8,128)S(1)} %get-tuple-element.19), channel_id=1, source_target_pairs={{0,112},{16,32},{32,16},{48,64},{64,48},{80,96},{96,80},{112,0},{1... | collective-permute-start | bytes 1769480 | tf_op jit(solution)/shard_map/ppermute | solution.py:33
where the time goes:
time: 57.4 us; the launch traced here: 57.3 us
  blocking collectives  19.3 us (34%)
  Pallas kernels  14.9 us (26%)
  waiting for transfers between devices  12.5 us (22%)
  starting transfers between devices  9.95 us (17%)
  between operations  0.65 us (1%)
    all_to_all x1, blocking collectives, on_device(): gathered = lax.all_to_all(packed, ('wide', 'narrow'), 0, 0, tiled=True)  19.3 us
    ppermute x4, waiting for transfers between devices, exchange(): return (lax.ppermute(first, axis, inner), lax.ppermute(second, axis, outer))  12.5 us
    pallas_call x1, Pallas kernels, basis_and_factor(): pl.pallas_call(lambda *refs: basis_kernel(last, long_y, *refs), out_shape...  11.1 us
    ppermute x4, starting transfers between devices, exchange(): return (lax.ppermute(first, axis, inner), lax.ppermute(second, axis, outer))  9.95 us
    pallas_call x1, Pallas kernels, combine(): pl.pallas_call(combine_kernel, out_shape=(block, block, jax.ShapeDtypeStr...  2.33 us
    pallas_call x1, Pallas kernels, edges(): pl.pallas_call(edge_kernel, out_shape=(shape, shape, whole), in_specs=[pl...  1.4 us
  transfers between devices with their start and end apart: 4, of which 2 were waited for; matrix products, arithmetic and copies ran while one was open for 0% of the time, Pallas kernels for 0%

commit v1 on v0

--- a/solution.py
+++ b/solution.py
@@ -37,64 +37,67 @@
     return [pl.BlockSpec(memory_space=pltpu.VMEM)] * count
 
 
-def edge_kernel(source, conduct, storage, inner, outer, own, sems):
-    odd = is_odd("narrow")
-    width = source.shape[1]
-
-    def fill(low, high):
-        copies = []
+def edge_kernel(source, conduct, storage, inner, outer, near, far, sems):
+    odd_n, odd_w = is_odd("narrow"), is_odd("wide")
+    size_x, width, _ = source.shape
+    half = size_x // 2
+
+    def copies(low, high, first, second):
+        result = []
         for k, ref in enumerate((source, conduct, storage)):
-            for side, (at, out) in enumerate(((0, low), (width - HALO, high))):
-                copies.append(
-                    pltpu.make_async_copy(
-                        ref.at[:, pl.ds(at, HALO), :], out.at[k], sems.at[2 * k + side]
-                    )
-                )
-            copies.append(pltpu.make_async_copy(ref, own.at[k], sems.at[6 + k]))
-        for copy in copies:
-            copy.start()
-        for copy in copies:
-            copy.wait()
-
-    @pl.when(odd)
-    def _():
-        fill(inner, outer)
-
-    @pl.when(jnp.logical_not(odd))
-    def _():
-        fill(outer, inner)
+            result += [
+                pltpu.make_async_copy(ref.at[:, pl.ds(0, HALO), :], low.at[k], sems.at[k]),
+                pltpu.make_async_copy(
+                    ref.at[:, pl.ds(width - HALO, HALO), :], high.at[k], sems.at[3 + k]
+                ),
+                pltpu.make_async_copy(ref.at[pl.ds(0, half)], first.at[k], sems.at[6 + k]),
+                pltpu.make_async_copy(ref.at[pl.ds(half, half)], second.at[k], sems.at[9 + k]),
+            ]
+        return result
+
+    for flag_n in (False, True):
+        for flag_w in (False, True):
+
+            @pl.when(jnp.logical_and(odd_n == flag_n, odd_w == flag_w))
+            def _(flag_n=flag_n, flag_w=flag_w):
+                rows = (inner, outer) if flag_n else (outer, inner)
+                halves = (near, far) if flag_w else (far, near)
+                every = copies(*rows, *halves)
+                for copy in every:
+                    copy.start()
+                for copy in every:
+                    copy.wait()
 
 
 def edges(source, conduct, storage):
-    size_x, _, size_z = source.shape
-    shape = jax.ShapeDtypeStruct((3, size_x, HALO, size_z), jnp.float32)
-    whole = jax.ShapeDtypeStruct((3, *source.shape), jnp.float32)
+    size_x, width, size_z = source.shape
+    rows = jax.ShapeDtypeStruct((3, size_x, HALO, size_z), jnp.float32)
+    halves = jax.ShapeDtypeStruct((3, size_x // 2, width, size_z), jnp.float32)
     return pl.pallas_call(
         edge_kernel,
-        out_shape=(shape, shape, whole),
+        out_shape=(rows, rows, halves, halves),
         in_specs=[pl.BlockSpec(memory_space=pltpu.HBM)] * 3,
-        out_specs=tuple(vmem_spec(3)),
-        scratch_shapes=[pltpu.SemaphoreType.DMA((9,))],
+        out_specs=tuple(vmem_spec(4)),
+        scratch_shapes=[pltpu.SemaphoreType.DMA((12,))],
         compiler_params=pltpu.CompilerParams(vmem_limit_bytes=8 * MIB),
         name="edges",
     )(*(pltpu.with_memory_space_constraint(x, pltpu.HBM) for x in (source, conduct, storage)))
 
 
-def widen_kernel(last, own, inner, outer, near, far):
+def corner_kernel(inner, outer, near, far):
     odd_n, odd_w = is_odd("narrow"), is_odd("wide")
-    place = lax.axis_index("narrow")
-    keep_low = jnp.where(place == 0, 0.0, 1.0)
-    keep_high = jnp.where(place == last, 0.0, 1.0)
-    _, size_x, width, _ = own.shape
-    half = size_x // 2
+    half = near.shape[1]
+    row = lax.broadcasted_iota(jnp.int32, near.shape[2:], 0)
 
     def fill(low_rows, high_rows, low_half, high_half):
         for k in range(3):
-            for part, out in ((0, low_half), (1, high_half)):
-                cells = slice(part * half, (part + 1) * half)
-                out[k, :, 0:HALO, :] = low_rows[k, cells] * keep_low
-                out[k, :, HALO : HALO + width, :] = own[k, cells]
-                out[k, :, HALO + width :, :] = high_rows[k, cells] * keep_high
+            for p in range(half):
+                low_half[k, p] = jnp.where(
+                    row >= p + 1, low_rows[k, p], high_rows[k, half - 1 - p]
+                )
+                high_half[k, p] = jnp.where(
+                    row >= half - p, low_rows[k, half + p], high_rows[k, 2 * half - 1 - p]
+                )
 
     for flag_n in (False, True):
         for flag_w in (False, True):
@@ -106,18 +109,17 @@
                 fill(*rows, *halves)
 
 
-def widen(own, inner, outer):
-    _, size_x, width, size_z = own.shape
-    shape = jax.ShapeDtypeStruct((3, size_x // 2, width + 2 * HALO, size_z), jnp.float32)
-    last = lax.axis_size("narrow") - 1
+def corners(inner, outer):
+    _, size_x, rows, size_z = inner.shape
+    shape = jax.ShapeDtypeStruct((3, size_x // 2, rows, size_z), jnp.float32)
     return pl.pallas_call(
-        lambda *refs: widen_kernel(last, *refs),
+        corner_kernel,
         out_shape=(shape, shape),
-        in_specs=vmem_spec(3),
+        in_specs=vmem_spec(2),
         out_specs=tuple(vmem_spec(2)),
         compiler_params=pltpu.CompilerParams(vmem_limit_bytes=8 * MIB),
-        name="widen",
-    )(own, inner, outer)
+        name="corners",
+    )(inner, outer)
 
 
 def total(x):
@@ -125,8 +127,9 @@
 
 
 def basis_kernel(
-    last, long_y, near, far, inner, outer, basis, rows_out,
-    field, cond, diag, face_x, face_y, face_yp, face_z, face_zp,
+    last, long_y, near, far, rows_inner, rows_outer, planes_inner, planes_outer,
+    corner_inner, corner_outer, basis, rows_out,
+    cond, diag, face_x, face_y, face_yp, face_z, face_zp,
     back_a, front_a, back_b, front_b, work,
 ):
     odd_w = is_odd("wide")
@@ -135,8 +138,9 @@
     keep_right = jnp.where(place_w == last[0], 0.0, 1.0)
     keep_low = jnp.where(place_n == 0, 0.0, 1.0)
     keep_high = jnp.where(place_n == last[1], 0.0, 1.0)
-    size_z = field.shape[1]
-    long_x = field.shape[0] // long_y
+    field = basis.at[0]
+    size_z = diag.shape[1]
+    long_x = diag.shape[0] // long_y
     size_x, size_y = long_x - 2 * HALO, long_y - 2 * HALO
     shifts = newton_shifts()
 
@@ -146,22 +150,46 @@
             start = pl.multiple_of(start, 8)
         return pl.ds(start, count)
 
-    def place(parts):
-        start = 0
-        for part, keep in zip(parts, (keep_left, None, None, keep_right)):
-            rows = part.shape[1]
-            for k, (out, skip) in enumerate(((field, 0), (cond, long_y), (diag, 0))):
-                value = part[k]
-                out[pl.ds(start + skip, rows), :] = value if keep is None else value * keep
-            start += rows
+    targets = ((field, 0), (cond, long_y), (diag, 0))
+
+    def place_own(low, high, first, second):
+        half = size_x // 2
+        for k, (out, skip) in enumerate(targets):
+            for p in range(size_x):
+                start = skip + (HALO + p) * long_y
+                out[pl.ds(start, HALO), :] = low[k, p] * keep_low
+                own = first[k, p] if p < half else second[k, p - half]
+                out[pl.ds(start + HALO, size_y), :] = own
+                out[pl.ds(start + HALO + size_y, HALO), :] = high[k, p] * keep_high
+
+    def place_beside(first, planes, tiles, keep):
+        for k, (out, skip) in enumerate(targets):
+            for p in range(HALO):
+                start = skip + (first + p) * long_y
+                out[pl.ds(start, HALO), :] = tiles[k, p] * (keep * keep_low)
+                out[pl.ds(start + HALO, size_y), :] = planes[k, p] * keep
+                out[pl.ds(start + HALO + size_y, HALO), :] = tiles[k, HALO - 1 - p] * (
+                    keep * keep_high
+                )
+
+    odd_n = is_odd("narrow")
+    for flag_n in (False, True):
+        for flag_w in (False, True):
+
+            @pl.when(jnp.logical_and(odd_n == flag_n, odd_w == flag_w))
+            def _(flag_n=flag_n, flag_w=flag_w):
+                rows = (rows_inner, rows_outer) if flag_n else (rows_outer, rows_inner)
+                place_own(*rows, *((near, far) if flag_w else (far, near)))
 
     @pl.when(odd_w)
     def _():
-        place((inner, near, far, outer))
+        place_beside(0, planes_inner, corner_inner, keep_left)
+        place_beside(HALO + size_x, planes_outer, corner_outer, keep_right)
 
     @pl.when(jnp.logical_not(odd_w))
     def _():
-        place((outer, far, near, inner))
+        place_beside(0, planes_outer, corner_outer, keep_left)
+        place_beside(HALO + size_x, planes_inner, corner_inner, keep_right)
 
     empty = jnp.zeros((long_y, size_z), jnp.float32)
     cond[at(0), :] = empty
@@ -271,8 +299,10 @@
 
     turned = ((back_a, front_a), (back_b, front_b))
     for number in range(STEPS):
-        read = field if number == 0 else basis.at[number - 1]
-        step(number, read, *turned[number % 2], basis.at[number], *turned[(number + 1) % 2])
+        step(
+            number, basis.at[number], *turned[number % 2],
+            basis.at[number + 1], *turned[(number + 1) % 2],
+        )
 
     def own(x):
         return at(x + HALO, size_y, HALO)
@@ -286,7 +316,7 @@
     zero = jnp.zeros((8, size_z), jnp.float32)
 
     def first_dots(x, sums):
-        columns = [field[own(x), :]] + [basis[j, own(x), :] for j in range(STEPS)]
+        columns = [basis[j, own(x), :] for j in range(COLS)]
         return tuple(s + fold(columns[0] * c) for s, c in zip(sums, columns))
 
     sums = lax.fori_loop(0, size_x, first_dots, (zero,) * COLS)
@@ -307,7 +337,7 @@
             pivot = field[own(x), :] if k == 0 else work[k, x]
             columns = []
             for j in range(k + 1, COLS):
-                old = basis[j - 1, own(x), :] if k == 0 else work[j, x]
+                old = basis[j, own(x), :] if k == 0 else work[j, x]
                 new = old - ratio[j - k] * pivot
                 work[j, x] = new
                 columns.append(new)
@@ -318,27 +348,26 @@
     rows_out[...] = jnp.broadcast_to(packed, rows_out.shape)
 
 
-def basis_and_factor(near, far, inner, outer):
-    _, half, long_y, size_z = near.shape
-    size_x, size_y = 2 * half, long_y - 2 * HALO
-    long_x = size_x + 2 * HALO
+def basis_and_factor(*parts):
+    _, half, size_y, size_z = parts[0].shape
+    size_x = 2 * half
+    long_x, long_y = size_x + 2 * HALO, size_y + 2 * HALO
     devices = lax.axis_size("wide") * lax.axis_size("narrow")
     last = (lax.axis_size("wide") - 1, lax.axis_size("narrow") - 1)
-    flat = lambda x: x.reshape(3, half * long_y, size_z)
     planes = lambda count: pltpu.VMEM((count * long_y, size_z), jnp.float32)
     return pl.pallas_call(
         lambda *refs: basis_kernel(last, long_y, *refs),
         out_shape=(
-            jax.ShapeDtypeStruct((STEPS, long_x * long_y, size_z), jnp.float32),
+            jax.ShapeDtypeStruct((COLS, long_x * long_y, size_z), jnp.float32),
             jax.ShapeDtypeStruct((devices, 128), jnp.float32),
         ),
-        in_specs=vmem_spec(4),
+        in_specs=vmem_spec(8),
         out_specs=tuple(vmem_spec(2)),
-        scratch_shapes=[planes(long_x), planes(long_x + 2)] + [planes(long_x)] * 10
+        scratch_shapes=[planes(long_x + 2)] + [planes(long_x)] * 10
         + [pltpu.VMEM((COLS, size_x, size_y, size_z), jnp.float32)],
         compiler_params=pltpu.CompilerParams(vmem_limit_bytes=28 * MIB),
         name="basis_and_factor",
-    )(flat(near), flat(far), flat(inner), flat(outer))
+    )(*parts)
 
 
 def split(x):
@@ -403,7 +432,7 @@
     return y, 1.0 / jnp.sqrt(square), z
 
 
-def combine_kernel(own, basis, rows, correction, remainder, upper, norm):
+def combine_kernel(basis, rows, correction, remainder, upper, norm):
     stacked = rows[...].T
     tops = [stacked[8 * j : 8 * j + 8] for j in range(COLS)]
     tail = stacked[8 * COLS : 8 * COLS + 8]
@@ -433,14 +462,15 @@
     upper[...] = table[:COLS, :COLS]
     norm[...] = size
 
-    _, size_x, size_y, _ = own.shape
+    size_x, size_y, _ = correction.shape
     long_y = size_y + 2 * HALO
 
     def combine(x, _):
-        here = own[0, x]
+        rows = pl.ds(pl.multiple_of((x + HALO) * long_y + HALO, 8), size_y)
+        here = basis[0, rows, :]
         first, second = y[0] * here, z[0] * here
         for j in range(1, COLS):
-            here = basis[j - 1, pl.ds(pl.multiple_of((x + HALO) * long_y + HALO, 8), size_y), :]
+            here = basis[j, rows, :]
             if j < STEPS:
                 first = first + y[j] * here
             second = second + z[j] * here
@@ -451,8 +481,8 @@
     lax.fori_loop(0, size_x, combine, 0)
 
 
-def combine(own, basis, rows):
-    block = jax.ShapeDtypeStruct(own.shape[1:], jnp.float32)
+def combine(shape, basis, rows):
+    block = jax.ShapeDtypeStruct(shape, jnp.float32)
     return pl.pallas_call(
         combine_kernel,
         out_shape=(
@@ -461,20 +491,21 @@
             jax.ShapeDtypeStruct((COLS, COLS), jnp.float32),
             jax.ShapeDtypeStruct((1, 1), jnp.float32),
         ),
-        in_specs=vmem_spec(3),
+        in_specs=vmem_spec(2),
         out_specs=tuple(vmem_spec(4)),
         compiler_params=pltpu.CompilerParams(vmem_limit_bytes=8 * MIB),
         name="combine",
-    )(own, basis, rows)
+    )(basis, rows)
 
 
 def on_device(source, conduct, storage):
-    inner, outer, own = edges(source, conduct, storage)
-    near, far = widen(own, *exchange(inner, outer, "narrow"))
+    inner, outer, near, far = edges(source, conduct, storage)
+    rows = exchange(inner, outer, "narrow")
     planes = exchange(near, far, "wide")
-    basis, packed = basis_and_factor(near, far, *planes)
+    tiles = exchange(*corners(*rows), "wide")
+    basis, packed = basis_and_factor(near, far, *rows, *planes, *tiles)
     gathered = lax.all_to_all(packed, ("wide", "narrow"), 0, 0, tiled=True)
-    correction, remainder, factor, resid = combine(own, basis, gathered)
+    correction, remainder, factor, resid = combine(source.shape, basis, gathered)
     return correction, remainder, factor, resid[0, 0]
 
 

time: 57.4 us -> 52.8 us (0.920)
  waiting for transfers between devices: 12.5 us -> 7.96 us
  blocking collectives: 19.3 us -> 16.5 us
  starting transfers between devices: 9.95 us -> 12.7 us
    ppermute x4 -> x6, waiting for transfers between devices: 12.5 us -> 7.96 us  [exchange(): return (lax.ppermute(first, axis, inner), lax.ppermute(second, axis, outer))]
    all_to_all x1, blocking collectives: 19.3 us -> 16.5 us  [on_device(): gathered = lax.all_to_all(packed, ('wide', 'narrow'), 0, 0, tiled=True)]
    ppermute x4 -> x6, starting transfers between devices: 9.95 us -> 12.7 us  [exchange(): return (lax.ppermute(first, axis, inner), lax.ppermute(second, axis, outer))]
  transfers between devices with their start and end apart: 4 -> 6, of which waited for: 2 -> 3; matrix products, arithmetic and copies ran while one was open for 0% -> 0% of each run, Pallas kernels for 0% -> 0%
where the time goes in v1:
time: 52.8 us; the launch traced here: 52.7 us
  blocking collectives  16.5 us (31%)
  Pallas kernels  14.9 us (28%)
  starting transfers between devices  12.7 us (24%)
  waiting for transfers between devices  7.96 us (15%)
  between operations  0.65 us (1%)
    all_to_all x1, blocking collectives, on_device(): gathered = lax.all_to_all(packed, ('wide', 'narrow'), 0, 0, tiled=True)  16.5 us
    ppermute x6, starting transfers between devices, exchange(): return (lax.ppermute(first, axis, inner), lax.ppermute(second, axis, outer))  12.7 us
    pallas_call x1, Pallas kernels, basis_and_factor(): pl.pallas_call(lambda *refs: basis_kernel(last, long_y, *refs), out_shape...  11.1 us
    ppermute x6, waiting for transfers between devices, exchange(): return (lax.ppermute(first, axis, inner), lax.ppermute(second, axis, outer))  7.96 us
    pallas_call x1, Pallas kernels, combine(): pl.pallas_call(combine_kernel, out_shape=(block, block, jax.ShapeDtypeStr...  2.34 us
    pallas_call x1, Pallas kernels, edges(): pl.pallas_call(edge_kernel, out_shape=(rows, rows, halves, halves), in_sp...  1.48 us
  transfers between devices with their start and end apart: 6, of which 3 were waited for; matrix products, arithmetic and copies ran while one was open for 0% of the time, Pallas kernels for 0%

profile of v1, /device:TPU:1, one launch (start us, length us, event | category | flops | bytes accessed | tf_op | source)
XLA Modules:
  0.0 52.7 jit_solution(16672802915490043302)
XLA Ops:
  0.6 1.5 %edges.1 = (f32[3,16,8,128]{3,2,1,0:T(8,128)S(1)}, f32[3,16,8,128]{3,2,1,0:T(8,128)S(1)}, f32[3,8,32,128]{3,2,1,0:T(8,128)S(1)}, f32[3,8,32,128]{3,2,1,0:T(8,128)S(1)}) custom-call(f32[16,32,128]{2,1,0:T(8,128)} %source.1, f32[16,32,128]{2,1,0:T(8,128)} %conduct.1, f32[16,32,128]{2,1,0:T(8,128)} %storage.1), custom_call_target="tpu_custom_call" | custom-call | tf_op jit(solution)/shard_map/edges/pallas_call | solution.py:76
  2.1 1.5 %collective-permute-start.2 = (f32[3,8,32,128]{3,2,1,0:T(8,128)S(1)}, f32[3,8,32,128]{3,2,1,0:T(8,128)S(1)}, u32[]{:S(2)}, u32[]{:S(2)}) collective-permute-start(f32[3,8,32,128]{3,2,1,0:T(8,128)S(1)} %get-tuple-element.16.refs_0_), channel_id=1, source_target_pairs={{0,16},{16,0},{32,48},{48,32},{64,80},{80,64},{96,112},{112,96},{1... | collective-permute-start | bytes 1179656 | tf_op jit(solution)/shard_map/ppermute | solution.py:33
  3.6 1.7 %collective-permute-start.3 = (f32[3,8,32,128]{3,2,1,0:T(8,128)S(1)}, f32[3,8,32,128]{3,2,1,0:T(8,128)S(1)}, u32[]{:S(2)}, u32[]{:S(2)}) collective-permute-start(f32[3,8,32,128]{3,2,1,0:T(8,128)S(1)} %get-tuple-element.17.refs_1_), channel_id=1, source_target_pairs={{0,112},{16,32},{32,16},{48,64},{64,48},{80,96},{96,80},{112,0},{1... | collective-permute-start | bytes 1179656 | tf_op jit(solution)/shard_map/ppermute | solution.py:33
  5.3 1.3 %collective-permute-start = (f32[3,16,8,128]{3,2,1,0:T(8,128)S(1)}, f32[3,16,8,128]{3,2,1,0:T(8,128)S(1)}, u32[]{:S(2)}, u32[]{:S(2)}) collective-permute-start(f32[3,16,8,128]{3,2,1,0:T(8,128)S(1)} %get-tuple-element.18), channel_id=1, source_target_pairs={{0,1},{1,0},{2,3},{3,2},{4,5},{5,4},{6,7},{7,6},{8,9},{9,8},{10,11... | collective-permute-start | bytes 589832 | tf_op jit(solution)/shard_map/ppermute | solution.py:33
  6.6 4.2 %collective-permute-start.1 = (f32[3,16,8,128]{3,2,1,0:T(8,128)S(1)}, f32[3,16,8,128]{3,2,1,0:T(8,128)S(1)}, u32[]{:S(2)}, u32[]{:S(2)}) collective-permute-start(f32[3,16,8,128]{3,2,1,0:T(8,128)S(1)} %get-tuple-element.19), channel_id=1, source_target_pairs={{0,15},{1,2},{2,1},{3,4},{4,3},{5,6},{6,5},{7,8},{8,7},{9,10},{10,... | collective-permute-start | bytes 589832 | tf_op jit(solution)/shard_map/ppermute | solution.py:33
  10.8 0.0 collective-permute-done.inner.refs_2_
  10.8 3.6 %collective-permute-done.1.outer.refs_3_ = f32[3,16,8,128]{3,2,1,0:T(8,128)S(1)} collective-permute-done((f32[3,16,8,128]{3,2,1,0:T(8,128)S(1)}, f32[3,16,8,128]{3,2,1,0:T(8,128)S(1)}, u32[]{:S(2)}, u32[]{:S(2)}) %collective-permute-start.1) | collective-permute-done | bytes 196640 | tf_op jit(solution)/shard_map/ppermute | solution.py:33
  14.4 4.1 %collective-permute-start.4 = (f32[3,8,8,128]{3,2,1,0:T(8,128)S(1)}, f32[3,8,8,128]{3,2,1,0:T(8,128)S(1)}, u32[]{:S(2)}, u32[]{:S(2)}) collective-permute-start(f32[3,8,8,128]{3,2,1,0:T(8,128)S(1)} %get-tuple-element.20), channel_id=1, source_target_pairs={{0,16},{16,0},{32,48},{48,32},{64,80},{80,64},{96,112},{112,96},{1... | collective-permute-start | bytes 294920 | tf_op jit(solution)/shard_map/ppermute | solution.py:33
  18.5 0.0 collective-permute-start.5
  18.5 0.9 %collective-permute-done.4.refs_6_ = f32[3,8,8,128]{3,2,1,0:T(8,128)S(1)} collective-permute-done((f32[3,8,8,128]{3,2,1,0:T(8,128)S(1)}, f32[3,8,8,128]{3,2,1,0:T(8,128)S(1)}, u32[]{:S(2)}, u32[]{:S(2)}) %collective-permute-start.4) | collective-permute-done | bytes 98336 | tf_op jit(solution)/shard_map/ppermute | solution.py:33
  19.4 3.4 %collective-permute-done.5.refs_7_ = f32[3,8,8,128]{3,2,1,0:T(8,128)S(1)} collective-permute-done((f32[3,8,8,128]{3,2,1,0:T(8,128)S(1)}, f32[3,8,8,128]{3,2,1,0:T(8,128)S(1)}, u32[]{:S(2)}, u32[]{:S(2)}) %collective-permute-start.5) | collective-permute-done | bytes 98336 | tf_op jit(solution)/shard_map/ppermute | solution.py:33
  22.8 0.0 collective-permute-done.2.refs_4_
  22.8 0.0 collective-permute-done.3.refs_5_
  22.8 11.1 %basis_and_factor.1 = (f32[9,1536,128]{2,1,0:T(8,128)S(1)}, f32[128,128]{1,0:T(8,128)S(1)}) custom-call(f32[3,8,32,128]{3,2,1,0:T(8,128)S(1)} %get-tuple-element.16.refs_0_, f32[3,8,32,128]{3,2,1,0:T(8,128)S(1)} %get-tuple-element.17.refs_1_, f32[3,16,8,128]{3,2,1,0:T(8,128)S(1)} %collective-permute-done.inner.refs_2_, ...), custom_call_target="tpu_custom_call" | custom-call | tf_op jit(solution)/shard_map/basis_and_factor/pallas_call | solution.py:358
  33.9 16.5 %all_to_all.11 = f32[128,1,128]{2,1,0:T(1,128)S(1)} all-to-all(f32[128,1,128]{2,1,0:T(1,128)S(1)} %bitcast.6), channel_id=1, replica_groups=mesh['wide'=8,'narrow'=16] {'wide','narrow'}, dimensions={0} | all-to-all | bytes 131072 | tf_op jit(solution)/shard_map/all_to_all | solution.py:507
  50.3 2.3 %combine.1 = (f32[16,32,128]{2,1,0:T(8,128)}, f32[16,32,128]{2,1,0:T(8,128)}, f32[9,9]{1,0:T(8,128)}, f32[1,1]{1,0:T(1,128)}) custom-call(f32[9,1536,128]{2,1,0:T(8,128)S(1)} %get-tuple-element.22.basis, f32[128,128]{1,0:T(8,128)S(1)} %bitcast.5), custom_call_target="tpu_custom_call" | custom-call | tf_op jit(solution)/shard_map/combine/pallas_call | solution.py:486
  (1 shorter events, 0.0 us)
Async XLA Ops:
  2.1 20.7 %collective-permute-start.2 = (f32[3,8,32,128]{3,2,1,0:T(8,128)S(1)}, f32[3,8,32,128]{3,2,1,0:T(8,128)S(1)}, u32[]{:S(2)}, u32[]{:S(2)}) collective-permute-start(f32[3,8,32,128]{3,2,1,0:T(8,128)S(1)} %get-tuple-element.16.refs_0_), channel_id=1, source_target_pairs={{0,16},{16,0},{32,48},{48,32},{64,80},{80,64},{96,112},{112,96},{1... | collective-permute-start | bytes 1179656 | tf_op jit(solution)/shard_map/ppermute | solution.py:33
  3.6 19.2 %collective-permute-start.3 = (f32[3,8,32,128]{3,2,1,0:T(8,128)S(1)}, f32[3,8,32,128]{3,2,1,0:T(8,128)S(1)}, u32[]{:S(2)}, u32[]{:S(2)}) collective-permute-start(f32[3,8,32,128]{3,2,1,0:T(8,128)S(1)} %get-tuple-element.17.refs_1_), channel_id=1, source_target_pairs={{0,112},{16,32},{32,16},{48,64},{64,48},{80,96},{96,80},{112,0},{1... | collective-permute-start | bytes 1179656 | tf_op jit(solution)/shard_map/ppermute | solution.py:33
  5.3 5.5 %collective-permute-start = (f32[3,16,8,128]{3,2,1,0:T(8,128)S(1)}, f32[3,16,8,128]{3,2,1,0:T(8,128)S(1)}, u32[]{:S(2)}, u32[]{:S(2)}) collective-permute-start(f32[3,16,8,128]{3,2,1,0:T(8,128)S(1)} %get-tuple-element.18), channel_id=1, source_target_pairs={{0,1},{1,0},{2,3},{3,2},{4,5},{5,4},{6,7},{7,6},{8,9},{9,8},{10,11... | collective-permute-start | bytes 589832 | tf_op jit(solution)/shard_map/ppermute | solution.py:33
  6.6 7.8 %collective-permute-start.1 = (f32[3,16,8,128]{3,2,1,0:T(8,128)S(1)}, f32[3,16,8,128]{3,2,1,0:T(8,128)S(1)}, u32[]{:S(2)}, u32[]{:S(2)}) collective-permute-start(f32[3,16,8,128]{3,2,1,0:T(8,128)S(1)} %get-tuple-element.19), channel_id=1, source_target_pairs={{0,15},{1,2},{2,1},{3,4},{4,3},{5,6},{6,5},{7,8},{8,7},{9,10},{10,... | collective-permute-start | bytes 589832 | tf_op jit(solution)/shard_map/ppermute | solution.py:33
  14.4 5.0 %collective-permute-start.4 = (f32[3,8,8,128]{3,2,1,0:T(8,128)S(1)}, f32[3,8,8,128]{3,2,1,0:T(8,128)S(1)}, u32[]{:S(2)}, u32[]{:S(2)}) collective-permute-start(f32[3,8,8,128]{3,2,1,0:T(8,128)S(1)} %get-tuple-element.20), channel_id=1, source_target_pairs={{0,16},{16,0},{32,48},{48,32},{64,80},{80,64},{96,112},{112,96},{1... | collective-permute-start | bytes 294920 | tf_op jit(solution)/shard_map/ppermute | solution.py:33
  18.5 4.3 %collective-permute-start.5 = (f32[3,8,8,128]{3,2,1,0:T(8,128)S(1)}, f32[3,8,8,128]{3,2,1,0:T(8,128)S(1)}, u32[]{:S(2)}, u32[]{:S(2)}) collective-permute-start(f32[3,8,8,128]{3,2,1,0:T(8,128)S(1)} %get-tuple-element.21), channel_id=1, source_target_pairs={{0,112},{16,32},{32,16},{48,64},{64,48},{80,96},{96,80},{112,0},{1... | collective-permute-start | bytes 294920 | tf_op jit(solution)/shard_map/ppermute | solution.py:33

commit v2 on v1

--- a/solution.py
+++ b/solution.py
@@ -233,7 +233,7 @@
         face_zp[at(x), :] = jnp.where(lane == size_z - 1, 0.0, z_high)
         diag[at(x), :] = unit * diag[at(x), :] + ((left + right) + (low + high) + (z_low + z_high))
 
-    group = 4
+    group = 16
 
     def start_group(g, _):
         for i in range(group):
@@ -249,6 +249,8 @@
         coefficients(long_x - group + i)
     face_x[at(HALO), :] = face_x[at(HALO), :] * keep_left
     face_x[at(HALO + size_x), :] = face_x[at(HALO + size_x), :] * keep_right
+
+    group = 12
 
     def step(number, read, back, front, write, next_back, next_front):
         theta = shifts[number] * unit
@@ -319,7 +321,7 @@
         columns = [basis[j, own(x), :] for j in range(COLS)]
         return tuple(s + fold(columns[0] * c) for s, c in zip(sums, columns))
 
-    sums = lax.fori_loop(0, size_x, first_dots, (zero,) * COLS)
+    sums = lax.fori_loop(0, size_x, first_dots, (zero,) * COLS, unroll=True)
     dots = [total(s) for s in sums]
     index = lax.broadcasted_iota(jnp.int32, (1, 128), 1)
     packed = jnp.zeros((1, 128), jnp.float32)
@@ -343,7 +345,9 @@
                 columns.append(new)
             return tuple(s + fold(columns[0] * c) for s, c in zip(sums, columns))
 
-        sums = lax.fori_loop(0, size_x, sweep, (zero,) * (COLS - 1 - k))
+        sums = lax.fori_loop(
+            0, size_x, sweep, (zero,) * (COLS - 1 - k), unroll=True
+        )
         dots = [total(s) for s in sums]
     rows_out[...] = jnp.broadcast_to(packed, rows_out.shape)
 
@@ -478,7 +482,7 @@
         remainder[x] = second
         return 0
 
-    lax.fori_loop(0, size_x, combine, 0)
+    lax.fori_loop(0, size_x, combine, 0, unroll=4)
 
 
 def combine(shape, basis, rows):

time: 52.8 us -> 47.2 us (0.89)
  Pallas kernels: 14.9 us -> 9.3 us
    pallas_call x1, Pallas kernels: 11.1 us -> 5.53 us  [basis_and_factor(): pl.pallas_call(lambda *refs: basis_kernel(last, long_y, *refs), out_shape...]
where the time goes in v2:
time: 47.2 us; the launch traced here: 47.1 us
  blocking collectives  16.5 us (35%)
  starting transfers between devices  12.7 us (27%)
  Pallas kernels  9.3 us (20%)
  waiting for transfers between devices  7.96 us (17%)
  between operations  0.66 us (1%)
    all_to_all x1, blocking collectives, on_device(): gathered = lax.all_to_all(packed, ('wide', 'narrow'), 0, 0, tiled=True)  16.5 us
    ppermute x6, starting transfers between devices, exchange(): return (lax.ppermute(first, axis, inner), lax.ppermute(second, axis, outer))  12.7 us
    ppermute x6, waiting for transfers between devices, exchange(): return (lax.ppermute(first, axis, inner), lax.ppermute(second, axis, outer))  7.96 us
    pallas_call x1, Pallas kernels, basis_and_factor(): pl.pallas_call(lambda *refs: basis_kernel(last, long_y, *refs), out_shape...  5.53 us
    pallas_call x1, Pallas kernels, combine(): pl.pallas_call(combine_kernel, out_shape=(block, block, jax.ShapeDtypeStr...  2.26 us
    pallas_call x1, Pallas kernels, edges(): pl.pallas_call(edge_kernel, out_shape=(rows, rows, halves, halves), in_sp...  1.48 us
  transfers between devices with their start and end apart: 6, of which 3 were waited for; matrix products, arithmetic and copies ran while one was open for 0% of the time, Pallas kernels for 0%

profile of v2, /device:TPU:1, one launch (start us, length us, event | category | flops | bytes accessed | tf_op | source)
XLA Modules:
  0.0 47.1 jit_solution(1384284374889376148)
XLA Ops:
  0.6 1.5 %edges.1 = (f32[3,16,8,128]{3,2,1,0:T(8,128)S(1)}, f32[3,16,8,128]{3,2,1,0:T(8,128)S(1)}, f32[3,8,32,128]{3,2,1,0:T(8,128)S(1)}, f32[3,8,32,128]{3,2,1,0:T(8,128)S(1)}) custom-call(f32[16,32,128]{2,1,0:T(8,128)} %source.1, f32[16,32,128]{2,1,0:T(8,128)} %conduct.1, f32[16,32,128]{2,1,0:T(8,128)} %storage.1), custom_call_target="tpu_custom_call" | custom-call | tf_op jit(solution)/shard_map/edges/pallas_call | solution.py:76
  2.1 1.5 %collective-permute-start.2 = (f32[3,8,32,128]{3,2,1,0:T(8,128)S(1)}, f32[3,8,32,128]{3,2,1,0:T(8,128)S(1)}, u32[]{:S(2)}, u32[]{:S(2)}) collective-permute-start(f32[3,8,32,128]{3,2,1,0:T(8,128)S(1)} %get-tuple-element.16.refs_0_), channel_id=1, source_target_pairs={{0,16},{16,0},{32,48},{48,32},{64,80},{80,64},{96,112},{112,96},{1... | collective-permute-start | bytes 1179656 | tf_op jit(solution)/shard_map/ppermute | solution.py:33
  3.6 1.7 %collective-permute-start.3 = (f32[3,8,32,128]{3,2,1,0:T(8,128)S(1)}, f32[3,8,32,128]{3,2,1,0:T(8,128)S(1)}, u32[]{:S(2)}, u32[]{:S(2)}) collective-permute-start(f32[3,8,32,128]{3,2,1,0:T(8,128)S(1)} %get-tuple-element.17.refs_1_), channel_id=1, source_target_pairs={{0,112},{16,32},{32,16},{48,64},{64,48},{80,96},{96,80},{112,0},{1... | collective-permute-start | bytes 1179656 | tf_op jit(solution)/shard_map/ppermute | solution.py:33
  5.3 1.3 %collective-permute-start = (f32[3,16,8,128]{3,2,1,0:T(8,128)S(1)}, f32[3,16,8,128]{3,2,1,0:T(8,128)S(1)}, u32[]{:S(2)}, u32[]{:S(2)}) collective-permute-start(f32[3,16,8,128]{3,2,1,0:T(8,128)S(1)} %get-tuple-element.18), channel_id=1, source_target_pairs={{0,1},{1,0},{2,3},{3,2},{4,5},{5,4},{6,7},{7,6},{8,9},{9,8},{10,11... | collective-permute-start | bytes 589832 | tf_op jit(solution)/shard_map/ppermute | solution.py:33
  6.6 4.2 %collective-permute-start.1 = (f32[3,16,8,128]{3,2,1,0:T(8,128)S(1)}, f32[3,16,8,128]{3,2,1,0:T(8,128)S(1)}, u32[]{:S(2)}, u32[]{:S(2)}) collective-permute-start(f32[3,16,8,128]{3,2,1,0:T(8,128)S(1)} %get-tuple-element.19), channel_id=1, source_target_pairs={{0,15},{1,2},{2,1},{3,4},{4,3},{5,6},{6,5},{7,8},{8,7},{9,10},{10,... | collective-permute-start | bytes 589832 | tf_op jit(solution)/shard_map/ppermute | solution.py:33
  10.8 0.0 collective-permute-done.inner.refs_2_
  10.8 3.6 %collective-permute-done.1.outer.refs_3_ = f32[3,16,8,128]{3,2,1,0:T(8,128)S(1)} collective-permute-done((f32[3,16,8,128]{3,2,1,0:T(8,128)S(1)}, f32[3,16,8,128]{3,2,1,0:T(8,128)S(1)}, u32[]{:S(2)}, u32[]{:S(2)}) %collective-permute-start.1) | collective-permute-done | bytes 196640 | tf_op jit(solution)/shard_map/ppermute | solution.py:33
  14.4 4.1 %collective-permute-start.4 = (f32[3,8,8,128]{3,2,1,0:T(8,128)S(1)}, f32[3,8,8,128]{3,2,1,0:T(8,128)S(1)}, u32[]{:S(2)}, u32[]{:S(2)}) collective-permute-start(f32[3,8,8,128]{3,2,1,0:T(8,128)S(1)} %get-tuple-element.20), channel_id=1, source_target_pairs={{0,16},{16,0},{32,48},{48,32},{64,80},{80,64},{96,112},{112,96},{1... | collective-permute-start | bytes 294920 | tf_op jit(solution)/shard_map/ppermute | solution.py:33
  18.5 0.0 collective-permute-start.5
  18.5 0.9 %collective-permute-done.4.refs_6_ = f32[3,8,8,128]{3,2,1,0:T(8,128)S(1)} collective-permute-done((f32[3,8,8,128]{3,2,1,0:T(8,128)S(1)}, f32[3,8,8,128]{3,2,1,0:T(8,128)S(1)}, u32[]{:S(2)}, u32[]{:S(2)}) %collective-permute-start.4) | collective-permute-done | bytes 98336 | tf_op jit(solution)/shard_map/ppermute | solution.py:33
  19.4 3.4 %collective-permute-done.5.refs_7_ = f32[3,8,8,128]{3,2,1,0:T(8,128)S(1)} collective-permute-done((f32[3,8,8,128]{3,2,1,0:T(8,128)S(1)}, f32[3,8,8,128]{3,2,1,0:T(8,128)S(1)}, u32[]{:S(2)}, u32[]{:S(2)}) %collective-permute-start.5) | collective-permute-done | bytes 98336 | tf_op jit(solution)/shard_map/ppermute | solution.py:33
  22.8 0.0 collective-permute-done.2.refs_4_
  22.8 0.0 collective-permute-done.3.refs_5_
  22.8 5.5 %basis_and_factor.1 = (f32[9,1536,128]{2,1,0:T(8,128)S(1)}, f32[128,128]{1,0:T(8,128)S(1)}) custom-call(f32[3,8,32,128]{3,2,1,0:T(8,128)S(1)} %get-tuple-element.16.refs_0_, f32[3,8,32,128]{3,2,1,0:T(8,128)S(1)} %get-tuple-element.17.refs_1_, f32[3,16,8,128]{3,2,1,0:T(8,128)S(1)} %collective-permute-done.inner.refs_2_, ...), custom_call_target="tpu_custom_call" | custom-call | tf_op jit(solution)/shard_map/basis_and_factor/pallas_call | solution.py:362
  28.4 16.5 %all_to_all.11 = f32[128,1,128]{2,1,0:T(1,128)S(1)} all-to-all(f32[128,1,128]{2,1,0:T(1,128)S(1)} %bitcast.6), channel_id=1, replica_groups=mesh['wide'=8,'narrow'=16] {'wide','narrow'}, dimensions={0} | all-to-all | bytes 131072 | tf_op jit(solution)/shard_map/all_to_all | solution.py:511
  44.8 2.3 %combine.1 = (f32[16,32,128]{2,1,0:T(8,128)}, f32[16,32,128]{2,1,0:T(8,128)}, f32[9,9]{1,0:T(8,128)}, f32[1,1]{1,0:T(1,128)}) custom-call(f32[9,1536,128]{2,1,0:T(8,128)S(1)} %get-tuple-element.22.basis, f32[128,128]{1,0:T(8,128)S(1)} %bitcast.5), custom_call_target="tpu_custom_call" | custom-call | tf_op jit(solution)/shard_map/combine/pallas_call | solution.py:490
  (1 shorter events, 0.0 us)
Async XLA Ops:
  2.1 20.7 %collective-permute-start.2 = (f32[3,8,32,128]{3,2,1,0:T(8,128)S(1)}, f32[3,8,32,128]{3,2,1,0:T(8,128)S(1)}, u32[]{:S(2)}, u32[]{:S(2)}) collective-permute-start(f32[3,8,32,128]{3,2,1,0:T(8,128)S(1)} %get-tuple-element.16.refs_0_), channel_id=1, source_target_pairs={{0,16},{16,0},{32,48},{48,32},{64,80},{80,64},{96,112},{112,96},{1... | collective-permute-start | bytes 1179656 | tf_op jit(solution)/shard_map/ppermute | solution.py:33
  3.6 19.2 %collective-permute-start.3 = (f32[3,8,32,128]{3,2,1,0:T(8,128)S(1)}, f32[3,8,32,128]{3,2,1,0:T(8,128)S(1)}, u32[]{:S(2)}, u32[]{:S(2)}) collective-permute-start(f32[3,8,32,128]{3,2,1,0:T(8,128)S(1)} %get-tuple-element.17.refs_1_), channel_id=1, source_target_pairs={{0,112},{16,32},{32,16},{48,64},{64,48},{80,96},{96,80},{112,0},{1... | collective-permute-start | bytes 1179656 | tf_op jit(solution)/shard_map/ppermute | solution.py:33
  5.3 5.5 %collective-permute-start = (f32[3,16,8,128]{3,2,1,0:T(8,128)S(1)}, f32[3,16,8,128]{3,2,1,0:T(8,128)S(1)}, u32[]{:S(2)}, u32[]{:S(2)}) collective-permute-start(f32[3,16,8,128]{3,2,1,0:T(8,128)S(1)} %get-tuple-element.18), channel_id=1, source_target_pairs={{0,1},{1,0},{2,3},{3,2},{4,5},{5,4},{6,7},{7,6},{8,9},{9,8},{10,11... | collective-permute-start | bytes 589832 | tf_op jit(solution)/shard_map/ppermute | solution.py:33
  6.6 7.8 %collective-permute-start.1 = (f32[3,16,8,128]{3,2,1,0:T(8,128)S(1)}, f32[3,16,8,128]{3,2,1,0:T(8,128)S(1)}, u32[]{:S(2)}, u32[]{:S(2)}) collective-permute-start(f32[3,16,8,128]{3,2,1,0:T(8,128)S(1)} %get-tuple-element.19), channel_id=1, source_target_pairs={{0,15},{1,2},{2,1},{3,4},{4,3},{5,6},{6,5},{7,8},{8,7},{9,10},{10,... | collective-permute-start | bytes 589832 | tf_op jit(solution)/shard_map/ppermute | solution.py:33
  14.4 5.0 %collective-permute-start.4 = (f32[3,8,8,128]{3,2,1,0:T(8,128)S(1)}, f32[3,8,8,128]{3,2,1,0:T(8,128)S(1)}, u32[]{:S(2)}, u32[]{:S(2)}) collective-permute-start(f32[3,8,8,128]{3,2,1,0:T(8,128)S(1)} %get-tuple-element.20), channel_id=1, source_target_pairs={{0,16},{16,0},{32,48},{48,32},{64,80},{80,64},{96,112},{112,96},{1... | collective-permute-start | bytes 294920 | tf_op jit(solution)/shard_map/ppermute | solution.py:33
  18.5 4.3 %collective-permute-start.5 = (f32[3,8,8,128]{3,2,1,0:T(8,128)S(1)}, f32[3,8,8,128]{3,2,1,0:T(8,128)S(1)}, u32[]{:S(2)}, u32[]{:S(2)}) collective-permute-start(f32[3,8,8,128]{3,2,1,0:T(8,128)S(1)} %get-tuple-element.21), channel_id=1, source_target_pairs={{0,112},{16,32},{32,16},{48,64},{64,48},{80,96},{96,80},{112,0},{1... | collective-permute-start | bytes 294920 | tf_op jit(solution)/shard_map/ppermute | solution.py:33

commit v3 on v2

--- a/solution.py
+++ b/solution.py
@@ -26,11 +26,24 @@
     return lax.rem(lax.axis_index(axis), 2) == 1
 
 
-def exchange(first, second, axis):
-    size = lax.axis_size(axis)
-    inner = [(i, i ^ 1) for i in range(size)]
-    outer = [(i, (((i + 1) % size ^ 1) - 1) % size) for i in range(size)]
-    return lax.ppermute(first, axis, inner), lax.ppermute(second, axis, outer)
+def swap(block, axis, shift):
+    axes = ("wide", "narrow")
+    sizes = [lax.axis_size(name) for name in axes]
+    along = axes.index(axis)
+    pairs = []
+    for i in range(sizes[0]):
+        for j in range(sizes[1]):
+            to = [i, j]
+            to[along] = (to[along] + shift ^ 1) - shift
+            if not 0 <= to[along] < sizes[along]:
+                to = [i, j]
+                to[1 - along] ^= 1
+            pairs.append((i * sizes[1] + j, to[0] * sizes[1] + to[1]))
+    return lax.ppermute(block, axes, pairs)
+
+
+def exchange(inner, outer, axis):
+    return swap(inner, axis, 0), swap(outer, axis, 1)
 
 
 def vmem_spec(count):
@@ -84,18 +97,21 @@
     )(*(pltpu.with_memory_space_constraint(x, pltpu.HBM) for x in (source, conduct, storage)))
 
 
-def corner_kernel(inner, outer, near, far):
+def corner_kernel(inner, outer, own, _, near, far):
     odd_n, odd_w = is_odd("narrow"), is_odd("wide")
     half = near.shape[1]
-    row = lax.broadcasted_iota(jnp.int32, near.shape[2:], 0)
+    row = lax.broadcasted_iota(jnp.int32, far.shape[2:], 0)
+    for k in range(3):
+        for p in range(half):
+            near[k, p, HALO:, :] = own[k, p]
 
     def fill(low_rows, high_rows, low_half, high_half):
         for k in range(3):
             for p in range(half):
-                low_half[k, p] = jnp.where(
+                low_half[k, p, 0:HALO, :] = jnp.where(
                     row >= p + 1, low_rows[k, p], high_rows[k, half - 1 - p]
                 )
-                high_half[k, p] = jnp.where(
+                high_half[k, p, 0:HALO, :] = jnp.where(
                     row >= half - p, low_rows[k, half + p], high_rows[k, 2 * half - 1 - p]
                 )
 
@@ -109,17 +125,17 @@
                 fill(*rows, *halves)
 
 
-def corners(inner, outer):
+def corners(inner, outer, own, wait):
     _, size_x, rows, size_z = inner.shape
-    shape = jax.ShapeDtypeStruct((3, size_x // 2, rows, size_z), jnp.float32)
+    shape = lambda count: jax.ShapeDtypeStruct((3, size_x // 2, count, size_z), jnp.float32)
     return pl.pallas_call(
         corner_kernel,
-        out_shape=(shape, shape),
-        in_specs=vmem_spec(2),
+        out_shape=(shape(rows + own.shape[2]), shape(rows)),
+        in_specs=vmem_spec(4),
         out_specs=tuple(vmem_spec(2)),
         compiler_params=pltpu.CompilerParams(vmem_limit_bytes=8 * MIB),
         name="corners",
-    )(inner, outer)
+    )(inner, outer, own, wait)
 
 
 def total(x):
@@ -128,7 +144,7 @@
 
 def basis_kernel(
     last, long_y, near, far, rows_inner, rows_outer, planes_inner, planes_outer,
-    corner_inner, corner_outer, basis, rows_out,
+    corner_outer, basis, rows_out,
     cond, diag, face_x, face_y, face_yp, face_z, face_zp,
     back_a, front_a, back_b, front_b, work,
 ):
@@ -166,11 +182,12 @@
         for k, (out, skip) in enumerate(targets):
             for p in range(HALO):
                 start = skip + (first + p) * long_y
-                out[pl.ds(start, HALO), :] = tiles[k, p] * (keep * keep_low)
-                out[pl.ds(start + HALO, size_y), :] = planes[k, p] * keep
-                out[pl.ds(start + HALO + size_y, HALO), :] = tiles[k, HALO - 1 - p] * (
-                    keep * keep_high
-                )
+                own = planes[k, p, planes.shape[2] - size_y :, :]
+                out[pl.ds(start, HALO), :] = tiles[k, p, 0:HALO, :] * (keep * keep_low)
+                out[pl.ds(start + HALO, size_y), :] = own * keep
+                out[pl.ds(start + HALO + size_y, HALO), :] = tiles[
+                    k, HALO - 1 - p, 0:HALO, :
+                ] * (keep * keep_high)
 
     odd_n = is_odd("narrow")
     for flag_n in (False, True):
@@ -183,13 +200,13 @@
 
     @pl.when(odd_w)
     def _():
-        place_beside(0, planes_inner, corner_inner, keep_left)
+        place_beside(0, planes_inner, planes_inner, keep_left)
         place_beside(HALO + size_x, planes_outer, corner_outer, keep_right)
 
     @pl.when(jnp.logical_not(odd_w))
     def _():
         place_beside(0, planes_outer, corner_outer, keep_left)
-        place_beside(HALO + size_x, planes_inner, corner_inner, keep_right)
+        place_beside(HALO + size_x, planes_inner, planes_inner, keep_right)
 
     empty = jnp.zeros((long_y, size_z), jnp.float32)
     cond[at(0), :] = empty
@@ -273,9 +290,10 @@
 
         def turn_plane(x):
             if not final:
-                here = write[at(x), :]
-                next_back[at(x), :] = pltpu.roll(here, 1, 1)
-                next_front[at(x), :] = pltpu.roll(here, size_z - 1, 1)
+                rows = at(x, size_y, HALO) if number == STEPS - 2 else at(x)
+                here = write[rows, :]
+                next_back[rows, :] = pltpu.roll(here, 1, 1)
+                next_front[rows, :] = pltpu.roll(here, size_z - 1, 1)
 
         start, stop = number + 1, long_x - 1 - number
         head = (stop - start) % group or group
@@ -365,7 +383,7 @@
             jax.ShapeDtypeStruct((COLS, long_x * long_y, size_z), jnp.float32),
             jax.ShapeDtypeStruct((devices, 128), jnp.float32),
         ),
-        in_specs=vmem_spec(8),
+        in_specs=vmem_spec(7),
         out_specs=tuple(vmem_spec(2)),
         scratch_shapes=[planes(long_x + 2)] + [planes(long_x)] * 10
         + [pltpu.VMEM((COLS, size_x, size_y, size_z), jnp.float32)],
@@ -505,9 +523,10 @@
 def on_device(source, conduct, storage):
     inner, outer, near, far = edges(source, conduct, storage)
     rows = exchange(inner, outer, "narrow")
-    planes = exchange(near, far, "wide")
-    tiles = exchange(*corners(*rows), "wide")
-    basis, packed = basis_and_factor(near, far, *rows, *planes, *tiles)
+    beyond = swap(far, "wide", 1)
+    near_all, far_tiles = corners(*rows, near, beyond)
+    tiles = exchange(near_all, far_tiles, "wide")
+    basis, packed = basis_and_factor(near, far, *rows, tiles[0], beyond, tiles[1])
     gathered = lax.all_to_all(packed, ("wide", "narrow"), 0, 0, tiled=True)
     correction, remainder, factor, resid = combine(source.shape, basis, gathered)
     return correction, remainder, factor, resid[0, 0]

time: 47.2 us -> 45.9 us (0.972)
  starting transfers between devices: 12.7 us -> 7.88 us
  waiting for transfers between devices: 7.96 us -> 9.99 us
  blocking collectives: 16.5 us -> 17.9 us
    ppermute x6 -> x5, starting transfers between devices: 12.7 us -> 7.88 us  [swap(): return lax.ppermute(block, axes, pairs)]
    ppermute x6 -> x5, waiting for transfers between devices: 7.96 us -> 9.99 us  [swap(): return lax.ppermute(block, axes, pairs)]
    all_to_all x1, blocking collectives: 16.5 us -> 17.9 us  [on_device(): gathered = lax.all_to_all(packed, ('wide', 'narrow'), 0, 0, tiled=True)]
  transfers between devices with their start and end apart: 6 -> 5, of which waited for: 3 -> 2; matrix products, arithmetic and copies ran while one was open for 0% -> 0% of each run, Pallas kernels for 0% -> 0%
where the time goes in v3:
time: 45.9 us; the launch traced here: 45.8 us
  blocking collectives  17.9 us (39%)
  waiting for transfers between devices  9.99 us (22%)
  Pallas kernels  9.33 us (20%)
  starting transfers between devices  7.88 us (17%)
  between operations  0.66 us (1%)
    all_to_all x1, blocking collectives, on_device(): gathered = lax.all_to_all(packed, ('wide', 'narrow'), 0, 0, tiled=True)  17.9 us
    ppermute x5, waiting for transfers between devices, swap(): return lax.ppermute(block, axes, pairs)  9.99 us
    ppermute x5, starting transfers between devices, swap(): return lax.ppermute(block, axes, pairs)  7.88 us
    pallas_call x1, Pallas kernels, basis_and_factor(): pl.pallas_call(lambda *refs: basis_kernel(last, long_y, *refs), out_shape...  5.53 us
    pallas_call x1, Pallas kernels, combine(): pl.pallas_call(combine_kernel, out_shape=(block, block, jax.ShapeDtypeStr...  2.26 us
    pallas_call x1, Pallas kernels, edges(): pl.pallas_call(edge_kernel, out_shape=(rows, rows, halves, halves), in_sp...  1.48 us
  transfers between devices with their start and end apart: 5, of which 2 were waited for; matrix products, arithmetic and copies ran while one was open for 0% of the time, Pallas kernels for 0%

profile of v3, /device:TPU:1, one launch (start us, length us, event | category | flops | bytes accessed | tf_op | source)
XLA Modules:
  0.0 45.8 jit_solution(12558624135007049982)
XLA Ops:
  0.6 1.5 %edges.1 = (f32[3,16,8,128]{3,2,1,0:T(8,128)S(1)}, f32[3,16,8,128]{3,2,1,0:T(8,128)S(1)}, f32[3,8,32,128]{3,2,1,0:T(8,128)S(1)}, f32[3,8,32,128]{3,2,1,0:T(8,128)S(1)}) custom-call(f32[16,32,128]{2,1,0:T(8,128)} %source.1, f32[16,32,128]{2,1,0:T(8,128)} %conduct.1, f32[16,32,128]{2,1,0:T(8,128)} %storage.1), custom_call_target="tpu_custom_call" | custom-call | tf_op jit(solution)/shard_map/edges/pallas_call | solution.py:89
  2.1 3.1 %collective-permute-start.2 = (f32[3,8,32,128]{3,2,1,0:T(8,128)S(1)}, f32[3,8,32,128]{3,2,1,0:T(8,128)S(1)}, u32[]{:S(2)}, u32[]{:S(2)}) collective-permute-start(f32[3,8,32,128]{3,2,1,0:T(8,128)S(1)} %get-tuple-element.17.refs_1_), channel_id=1, source_target_pairs={{0,1},{1,0},{2,3},{3,2},{4,5},{5,4},{6,7},{7,6},{8,9},{9,8},{10,11... | collective-permute-start | bytes 1179656 | tf_op jit(solution)/shard_map/ppermute | solution.py:42
  5.2 1.3 %collective-permute-start = (f32[3,16,8,128]{3,2,1,0:T(8,128)S(1)}, f32[3,16,8,128]{3,2,1,0:T(8,128)S(1)}, u32[]{:S(2)}, u32[]{:S(2)}) collective-permute-start(f32[3,16,8,128]{3,2,1,0:T(8,128)S(1)} %get-tuple-element.18), channel_id=1, source_target_pairs={{0,1},{1,0},{2,3},{3,2},{4,5},{5,4},{6,7},{7,6},{8,9},{9,8},{10,11... | collective-permute-start | bytes 589832 | tf_op jit(solution)/shard_map/ppermute | solution.py:42
  6.5 0.0 collective-permute-start.1
  6.5 5.7 %collective-permute-done.inner.refs_2_ = f32[3,16,8,128]{3,2,1,0:T(8,128)S(1)} collective-permute-done((f32[3,16,8,128]{3,2,1,0:T(8,128)S(1)}, f32[3,16,8,128]{3,2,1,0:T(8,128)S(1)}, u32[]{:S(2)}, u32[]{:S(2)}) %collective-permute-start) | collective-permute-done | bytes 196640 | tf_op jit(solution)/shard_map/ppermute | solution.py:42
  12.1 0.0 collective-permute-done.1.outer.refs_3_
  12.1 0.0 collective-permute-done.2._.refs_5_
  12.1 0.1 corners.1
  12.2 3.5 %collective-permute-start.3 = (f32[3,8,40,128]{3,2,1,0:T(8,128)S(1)}, f32[3,8,40,128]{3,2,1,0:T(8,128)S(1)}, u32[]{:S(2)}, u32[]{:S(2)}) collective-permute-start(f32[3,8,40,128]{3,2,1,0:T(8,128)S(1)} %get-tuple-element.20), channel_id=1, source_target_pairs={{0,16},{1,17},{2,18},{3,19},{4,20},{5,21},{6,22},{7,23},{8,24},{9,... | collective-permute-start | bytes 1474568 | tf_op jit(solution)/shard_map/ppermute | solution.py:42
  15.7 0.0 collective-permute-start.4
  15.7 4.3 %collective-permute-done.4.refs_6_ = f32[3,8,8,128]{3,2,1,0:T(8,128)S(1)} collective-permute-done((f32[3,8,8,128]{3,2,1,0:T(8,128)S(1)}, f32[3,8,8,128]{3,2,1,0:T(8,128)S(1)}, u32[]{:S(2)}, u32[]{:S(2)}) %collective-permute-start.4) | collective-permute-done | bytes 98336 | tf_op jit(solution)/shard_map/ppermute | solution.py:42
  20.1 0.0 collective-permute-done.3.refs_4_
  20.1 5.5 %basis_and_factor.1 = (f32[9,1536,128]{2,1,0:T(8,128)S(1)}, f32[128,128]{1,0:T(8,128)S(1)}) custom-call(f32[3,8,32,128]{3,2,1,0:T(8,128)S(1)} %get-tuple-element.16.own.refs_0_, f32[3,8,32,128]{3,2,1,0:T(8,128)S(1)} %get-tuple-element.17.refs_1_, f32[3,16,8,128]{3,2,1,0:T(8,128)S(1)} %collective-permute-done.inner.refs_2_, ...), custom_call_target="tpu_custom_call" | custom-call | tf_op jit(solution)/shard_map/basis_and_factor/pallas_call | solution.py:380
  25.6 17.9 %all_to_all.11 = f32[128,1,128]{2,1,0:T(1,128)S(1)} all-to-all(f32[128,1,128]{2,1,0:T(1,128)S(1)} %bitcast.6), channel_id=1, replica_groups=mesh['wide'=8,'narrow'=16] {'wide','narrow'}, dimensions={0} | all-to-all | bytes 131072 | tf_op jit(solution)/shard_map/all_to_all | solution.py:530
  43.5 2.3 %combine.1 = (f32[16,32,128]{2,1,0:T(8,128)}, f32[16,32,128]{2,1,0:T(8,128)}, f32[9,9]{1,0:T(8,128)}, f32[1,1]{1,0:T(1,128)}) custom-call(f32[9,1536,128]{2,1,0:T(8,128)S(1)} %get-tuple-element.22.basis, f32[128,128]{1,0:T(8,128)S(1)} %bitcast.5), custom_call_target="tpu_custom_call" | custom-call | tf_op jit(solution)/shard_map/combine/pallas_call | solution.py:508
Async XLA Ops:
  2.1 10.0 %collective-permute-start.2 = (f32[3,8,32,128]{3,2,1,0:T(8,128)S(1)}, f32[3,8,32,128]{3,2,1,0:T(8,128)S(1)}, u32[]{:S(2)}, u32[]{:S(2)}) collective-permute-start(f32[3,8,32,128]{3,2,1,0:T(8,128)S(1)} %get-tuple-element.17.refs_1_), channel_id=1, source_target_pairs={{0,1},{1,0},{2,3},{3,2},{4,5},{5,4},{6,7},{7,6},{8,9},{9,8},{10,11... | collective-permute-start | bytes 1179656 | tf_op jit(solution)/shard_map/ppermute | solution.py:42
  5.2 6.9 %collective-permute-start = (f32[3,16,8,128]{3,2,1,0:T(8,128)S(1)}, f32[3,16,8,128]{3,2,1,0:T(8,128)S(1)}, u32[]{:S(2)}, u32[]{:S(2)}) collective-permute-start(f32[3,16,8,128]{3,2,1,0:T(8,128)S(1)} %get-tuple-element.18), channel_id=1, source_target_pairs={{0,1},{1,0},{2,3},{3,2},{4,5},{5,4},{6,7},{7,6},{8,9},{9,8},{10,11... | collective-permute-start | bytes 589832 | tf_op jit(solution)/shard_map/ppermute | solution.py:42
  6.5 5.7 %collective-permute-start.1 = (f32[3,16,8,128]{3,2,1,0:T(8,128)S(1)}, f32[3,16,8,128]{3,2,1,0:T(8,128)S(1)}, u32[]{:S(2)}, u32[]{:S(2)}) collective-permute-start(f32[3,16,8,128]{3,2,1,0:T(8,128)S(1)} %get-tuple-element.19), channel_id=1, source_target_pairs={{0,16},{1,2},{2,1},{3,4},{4,3},{5,6},{6,5},{7,8},{8,7},{9,10},{10,... | collective-permute-start | bytes 589832 | tf_op jit(solution)/shard_map/ppermute | solution.py:42
  12.2 7.9 %collective-permute-start.3 = (f32[3,8,40,128]{3,2,1,0:T(8,128)S(1)}, f32[3,8,40,128]{3,2,1,0:T(8,128)S(1)}, u32[]{:S(2)}, u32[]{:S(2)}) collective-permute-start(f32[3,8,40,128]{3,2,1,0:T(8,128)S(1)} %get-tuple-element.20), channel_id=1, source_target_pairs={{0,16},{1,17},{2,18},{3,19},{4,20},{5,21},{6,22},{7,23},{8,24},{9,... | collective-permute-start | bytes 1474568 | tf_op jit(solution)/shard_map/ppermute | solution.py:42
  15.7 4.3 %collective-permute-start.4 = (f32[3,8,8,128]{3,2,1,0:T(8,128)S(1)}, f32[3,8,8,128]{3,2,1,0:T(8,128)S(1)}, u32[]{:S(2)}, u32[]{:S(2)}) collective-permute-start(f32[3,8,8,128]{3,2,1,0:T(8,128)S(1)} %get-tuple-element.21), channel_id=1, source_target_pairs={{0,1},{1,0},{2,3},{3,2},{4,5},{5,4},{6,7},{7,6},{8,9},{9,8},{10,11... | collective-permute-start | bytes 294920 | tf_op jit(solution)/shard_map/ppermute | solution.py:42

commit v4 on v3

--- a/solution.py
+++ b/solution.py
@@ -55,31 +55,28 @@
     size_x, width, _ = source.shape
     half = size_x // 2
 
-    def copies(low, high, first, second):
-        result = []
-        for k, ref in enumerate((source, conduct, storage)):
-            result += [
-                pltpu.make_async_copy(ref.at[:, pl.ds(0, HALO), :], low.at[k], sems.at[k]),
-                pltpu.make_async_copy(
-                    ref.at[:, pl.ds(width - HALO, HALO), :], high.at[k], sems.at[3 + k]
-                ),
-                pltpu.make_async_copy(ref.at[pl.ds(0, half)], first.at[k], sems.at[6 + k]),
-                pltpu.make_async_copy(ref.at[pl.ds(half, half)], second.at[k], sems.at[9 + k]),
-            ]
-        return result
-
     for flag_n in (False, True):
         for flag_w in (False, True):
 
             @pl.when(jnp.logical_and(odd_n == flag_n, odd_w == flag_w))
             def _(flag_n=flag_n, flag_w=flag_w):
-                rows = (inner, outer) if flag_n else (outer, inner)
+                low, high = (inner, outer) if flag_n else (outer, inner)
                 halves = (near, far) if flag_w else (far, near)
-                every = copies(*rows, *halves)
-                for copy in every:
+                copies = []
+                for k, ref in enumerate((source, conduct, storage)):
+                    for side, out in enumerate(halves):
+                        block = ref.at[pl.ds(side * half, half)]
+                        copies.append(
+                            pltpu.make_async_copy(block, out.at[k], sems.at[2 * k + side])
+                        )
+                for copy in copies:
                     copy.start()
-                for copy in every:
+                for copy in copies:
                     copy.wait()
+                for side, out in enumerate(halves):
+                    planes = pl.ds(side * half, half)
+                    low[:, planes] = out[:, :, 0:HALO, :]
+                    high[:, planes] = out[:, :, width - HALO : width, :]
 
 
 def edges(source, conduct, storage):
@@ -91,7 +88,7 @@
         out_shape=(rows, rows, halves, halves),
         in_specs=[pl.BlockSpec(memory_space=pltpu.HBM)] * 3,
         out_specs=tuple(vmem_spec(4)),
-        scratch_shapes=[pltpu.SemaphoreType.DMA((12,))],
+        scratch_shapes=[pltpu.SemaphoreType.DMA((6,))],
         compiler_params=pltpu.CompilerParams(vmem_limit_bytes=8 * MIB),
         name="edges",
     )(*(pltpu.with_memory_space_constraint(x, pltpu.HBM) for x in (source, conduct, storage)))
@@ -467,12 +464,14 @@
             square = square + tail * tail
         dots = [total(square)] + [total(tops[k] * tops[j]) for j in range(k + 1, COLS)]
         ridge = dots[0] + 1e-12
+        inverse = 1.0 / ridge
+        again = 2.0 - dots[0] * inverse
+        scale = inverse * again
         length = jnp.sqrt(ridge)
-        again = 2.0 - dots[0] / ridge
         factor[(k, k)] = length
         for j in range(k + 1, COLS):
-            factor[(k, j)] = dots[j - k] / length * again
-            tops[j] = tops[j] - (dots[j - k] / ridge * again) * tops[k]
+            tops[j] = tops[j] - (dots[j - k] * scale) * tops[k]
+            factor[(k, j)] = dots[j - k] * (length * scale)
 
     y, size, z = small_solve(factor)
 

time: 45.9 us -> 45.8 us (level)
  no operation moved by 1% of the time
where the time goes in v4:
time: 45.8 us; the launch traced here: 45.6 us
  blocking collectives  17.9 us (39%)
  waiting for transfers between devices  10 us (22%)
  Pallas kernels  9.17 us (20%)
  starting transfers between devices  7.86 us (17%)
  between operations  0.66 us (1%)
    all_to_all x1, blocking collectives, on_device(): gathered = lax.all_to_all(packed, ('wide', 'narrow'), 0, 0, tiled=True)  17.9 us
    ppermute x5, waiting for transfers between devices, swap(): return lax.ppermute(block, axes, pairs)  10 us
    ppermute x5, starting transfers between devices, swap(): return lax.ppermute(block, axes, pairs)  7.86 us
    pallas_call x1, Pallas kernels, basis_and_factor(): pl.pallas_call(lambda *refs: basis_kernel(last, long_y, *refs), out_shape...  5.53 us
    pallas_call x1, Pallas kernels, combine(): pl.pallas_call(combine_kernel, out_shape=(block, block, jax.ShapeDtypeStr...  2.27 us
    pallas_call x1, Pallas kernels, edges(): pl.pallas_call(edge_kernel, out_shape=(rows, rows, halves, halves), in_sp...  1.31 us
  transfers between devices with their start and end apart: 5, of which 2 were waited for; matrix products, arithmetic and copies ran while one was open for 0% of the time, Pallas kernels for 0%

profile of v4, /device:TPU:1, one launch (start us, length us, event | category | flops | bytes accessed | tf_op | source)
XLA Modules:
  0.0 45.6 jit_solution(8342358411134949622)
XLA Ops:
  0.6 1.3 %edges.1 = (f32[3,16,8,128]{3,2,1,0:T(8,128)S(1)}, f32[3,16,8,128]{3,2,1,0:T(8,128)S(1)}, f32[3,8,32,128]{3,2,1,0:T(8,128)S(1)}, f32[3,8,32,128]{3,2,1,0:T(8,128)S(1)}) custom-call(f32[16,32,128]{2,1,0:T(8,128)} %source.1, f32[16,32,128]{2,1,0:T(8,128)} %conduct.1, f32[16,32,128]{2,1,0:T(8,128)} %storage.1), custom_call_target="tpu_custom_call" | custom-call | tf_op jit(solution)/shard_map/edges/pallas_call | solution.py:86
  1.9 3.1 %collective-permute-start.2 = (f32[3,8,32,128]{3,2,1,0:T(8,128)S(1)}, f32[3,8,32,128]{3,2,1,0:T(8,128)S(1)}, u32[]{:S(2)}, u32[]{:S(2)}) collective-permute-start(f32[3,8,32,128]{3,2,1,0:T(8,128)S(1)} %get-tuple-element.17.refs_1_), channel_id=1, source_target_pairs={{0,1},{1,0},{2,3},{3,2},{4,5},{5,4},{6,7},{7,6},{8,9},{9,8},{10,11... | collective-permute-start | bytes 1179656 | tf_op jit(solution)/shard_map/ppermute | solution.py:42
  5.1 1.2 %collective-permute-start = (f32[3,16,8,128]{3,2,1,0:T(8,128)S(1)}, f32[3,16,8,128]{3,2,1,0:T(8,128)S(1)}, u32[]{:S(2)}, u32[]{:S(2)}) collective-permute-start(f32[3,16,8,128]{3,2,1,0:T(8,128)S(1)} %get-tuple-element.18), channel_id=1, source_target_pairs={{0,1},{1,0},{2,3},{3,2},{4,5},{5,4},{6,7},{7,6},{8,9},{9,8},{10,11... | collective-permute-start | bytes 589832 | tf_op jit(solution)/shard_map/ppermute | solution.py:42
  6.3 0.0 collective-permute-start.1
  6.3 5.7 %collective-permute-done.inner.refs_2_ = f32[3,16,8,128]{3,2,1,0:T(8,128)S(1)} collective-permute-done((f32[3,16,8,128]{3,2,1,0:T(8,128)S(1)}, f32[3,16,8,128]{3,2,1,0:T(8,128)S(1)}, u32[]{:S(2)}, u32[]{:S(2)}) %collective-permute-start) | collective-permute-done | bytes 196640 | tf_op jit(solution)/shard_map/ppermute | solution.py:42
  12.0 0.0 collective-permute-done.1.outer.refs_3_
  12.0 0.0 collective-permute-done.2._.refs_5_
  12.0 0.1 corners.1
  12.1 3.5 %collective-permute-start.3 = (f32[3,8,40,128]{3,2,1,0:T(8,128)S(1)}, f32[3,8,40,128]{3,2,1,0:T(8,128)S(1)}, u32[]{:S(2)}, u32[]{:S(2)}) collective-permute-start(f32[3,8,40,128]{3,2,1,0:T(8,128)S(1)} %get-tuple-element.20), channel_id=1, source_target_pairs={{0,16},{1,17},{2,18},{3,19},{4,20},{5,21},{6,22},{7,23},{8,24},{9,... | collective-permute-start | bytes 1474568 | tf_op jit(solution)/shard_map/ppermute | solution.py:42
  15.6 0.0 collective-permute-start.4
  15.6 4.3 %collective-permute-done.4.refs_6_ = f32[3,8,8,128]{3,2,1,0:T(8,128)S(1)} collective-permute-done((f32[3,8,8,128]{3,2,1,0:T(8,128)S(1)}, f32[3,8,8,128]{3,2,1,0:T(8,128)S(1)}, u32[]{:S(2)}, u32[]{:S(2)}) %collective-permute-start.4) | collective-permute-done | bytes 98336 | tf_op jit(solution)/shard_map/ppermute | solution.py:42
  19.9 0.0 collective-permute-done.3.refs_4_
  19.9 5.5 %basis_and_factor.1 = (f32[9,1536,128]{2,1,0:T(8,128)S(1)}, f32[128,128]{1,0:T(8,128)S(1)}) custom-call(f32[3,8,32,128]{3,2,1,0:T(8,128)S(1)} %get-tuple-element.16.own.refs_0_, f32[3,8,32,128]{3,2,1,0:T(8,128)S(1)} %get-tuple-element.17.refs_1_, f32[3,16,8,128]{3,2,1,0:T(8,128)S(1)} %collective-permute-done.inner.refs_2_, ...), custom_call_target="tpu_custom_call" | custom-call | tf_op jit(solution)/shard_map/basis_and_factor/pallas_call | solution.py:377
  25.4 17.9 %all_to_all.11 = f32[128,1,128]{2,1,0:T(1,128)S(1)} all-to-all(f32[128,1,128]{2,1,0:T(1,128)S(1)} %bitcast.6), channel_id=1, replica_groups=mesh['wide'=8,'narrow'=16] {'wide','narrow'}, dimensions={0} | all-to-all | bytes 131072 | tf_op jit(solution)/shard_map/all_to_all | solution.py:529
  43.3 2.3 %combine.1 = (f32[16,32,128]{2,1,0:T(8,128)}, f32[16,32,128]{2,1,0:T(8,128)}, f32[9,9]{1,0:T(8,128)}, f32[1,1]{1,0:T(1,128)}) custom-call(f32[9,1536,128]{2,1,0:T(8,128)S(1)} %get-tuple-element.22.basis, f32[128,128]{1,0:T(8,128)S(1)} %bitcast.5), custom_call_target="tpu_custom_call" | custom-call | tf_op jit(solution)/shard_map/combine/pallas_call | solution.py:507
Async XLA Ops:
  1.9 10.0 %collective-permute-start.2 = (f32[3,8,32,128]{3,2,1,0:T(8,128)S(1)}, f32[3,8,32,128]{3,2,1,0:T(8,128)S(1)}, u32[]{:S(2)}, u32[]{:S(2)}) collective-permute-start(f32[3,8,32,128]{3,2,1,0:T(8,128)S(1)} %get-tuple-element.17.refs_1_), channel_id=1, source_target_pairs={{0,1},{1,0},{2,3},{3,2},{4,5},{5,4},{6,7},{7,6},{8,9},{9,8},{10,11... | collective-permute-start | bytes 1179656 | tf_op jit(solution)/shard_map/ppermute | solution.py:42
  5.1 6.9 %collective-permute-start = (f32[3,16,8,128]{3,2,1,0:T(8,128)S(1)}, f32[3,16,8,128]{3,2,1,0:T(8,128)S(1)}, u32[]{:S(2)}, u32[]{:S(2)}) collective-permute-start(f32[3,16,8,128]{3,2,1,0:T(8,128)S(1)} %get-tuple-element.18), channel_id=1, source_target_pairs={{0,1},{1,0},{2,3},{3,2},{4,5},{5,4},{6,7},{7,6},{8,9},{9,8},{10,11... | collective-permute-start | bytes 589832 | tf_op jit(solution)/shard_map/ppermute | solution.py:42
  6.3 5.7 %collective-permute-start.1 = (f32[3,16,8,128]{3,2,1,0:T(8,128)S(1)}, f32[3,16,8,128]{3,2,1,0:T(8,128)S(1)}, u32[]{:S(2)}, u32[]{:S(2)}) collective-permute-start(f32[3,16,8,128]{3,2,1,0:T(8,128)S(1)} %get-tuple-element.19), channel_id=1, source_target_pairs={{0,16},{1,2},{2,1},{3,4},{4,3},{5,6},{6,5},{7,8},{8,7},{9,10},{10,... | collective-permute-start | bytes 589832 | tf_op jit(solution)/shard_map/ppermute | solution.py:42
  12.1 7.9 %collective-permute-start.3 = (f32[3,8,40,128]{3,2,1,0:T(8,128)S(1)}, f32[3,8,40,128]{3,2,1,0:T(8,128)S(1)}, u32[]{:S(2)}, u32[]{:S(2)}) collective-permute-start(f32[3,8,40,128]{3,2,1,0:T(8,128)S(1)} %get-tuple-element.20), channel_id=1, source_target_pairs={{0,16},{1,17},{2,18},{3,19},{4,20},{5,21},{6,22},{7,23},{8,24},{9,... | collective-permute-start | bytes 1474568 | tf_op jit(solution)/shard_map/ppermute | solution.py:42
  15.6 4.3 %collective-permute-start.4 = (f32[3,8,8,128]{3,2,1,0:T(8,128)S(1)}, f32[3,8,8,128]{3,2,1,0:T(8,128)S(1)}, u32[]{:S(2)}, u32[]{:S(2)}) collective-permute-start(f32[3,8,8,128]{3,2,1,0:T(8,128)S(1)} %get-tuple-element.21), channel_id=1, source_target_pairs={{0,1},{1,0},{2,3},{3,2},{4,5},{5,4},{6,7},{7,6},{8,9},{9,8},{10,11... | collective-permute-start | bytes 294920 | tf_op jit(solution)/shard_map/ppermute | solution.py:42
